TPU v7x, 32 devices: a whole 2x2x4 slice. The times are simulated.
32 devices in a mesh: dp: 16 (over z, x, core), mp: 2 (over y).
Axes of the slice: x: 2, y: 2, z: 4, core: 2. Of those that a mesh axis runs over, the one named last changes fastest.
Arguments:
- tokens: bfloat16 [24576, 768], P(('dp', 'mp')), may hold values from -6 to 6
- lengths: int32 [48, 4], P('dp'), may hold values from 0 to 512, as said below
- buckets: int32 [48], P('dp'), may hold values from 0 to 2, as said below
- w_query: bfloat16 [768, 768], P(None, 'mp'), may hold values from -0.3125 to 0.3125
- b_query: bfloat16 [768], P('mp'), may hold values from -2 to 2
- w_key: bfloat16 [768, 768], P(None, 'mp'), may hold values from -0.21875 to 0.21875
- w_value: bfloat16 [768, 768], P(None, 'mp'), may hold values from -0.21875 to 0.21875
- b_value: bfloat16 [768], P('mp'), may hold values from -1 to 1
- w_out: bfloat16 [768, 768], P('mp'), may hold values from -1.75 to 1.75
- b_out: bfloat16 [768], replicated, may hold values from -2 to 2
- norm1_gain: bfloat16 [768], replicated, may hold values from 0.5 to 1.5
- norm1_bias: bfloat16 [768], replicated, may hold values from -2 to 2
- w_up: bfloat16 [768, 3072], P(None, 'mp'), may hold values from -0.21875 to 0.21875
- b_up: bfloat16 [3072], P('mp'), may hold values from -2 to 2
- w_down: bfloat16 [3072, 768], P('mp'), may hold values from -0.109375 to 0.109375
- b_down: bfloat16 [768], replicated, may hold values from -2 to 2
- norm2_gain: bfloat16 [768], replicated, may hold values from 0.5 to 1.5
- norm2_bias: bfloat16 [768], replicated, may hold values from -2 to 2
- cotangent: bfloat16 [24576, 768], P(('dp', 'mp')), may hold values from -6 to 6
Outputs:
- output: bfloat16 [24576, 768], P(('dp', 'mp'))
- input_grad: float32 [24576, 768], P(('dp', 'mp'))
- w_query_grad: float32 [768, 768], P(None, 'mp')
- b_query_grad: float32 [768], P('mp')
- w_key_grad: float32 [768, 768], P(None, 'mp')
- w_value_grad: float32 [768, 768], P(None, 'mp')
- b_value_grad: float32 [768], P('mp')
- w_out_grad: float32 [768, 768], P('mp')
- b_out_grad: float32 [768], replicated
- norm1_gain_grad: float32 [768], replicated
- norm1_bias_grad: float32 [768], replicated
- w_up_grad: float32 [768, 3072], P(None, 'mp')
- b_up_grad: float32 [3072], P('mp')
- w_down_grad: float32 [3072, 768], P('mp')
- b_down_grad: float32 [768], replicated
- norm2_gain_grad: float32 [768], replicated
- norm2_bias_grad: float32 [768], replicated
Inputs may be any that keep to these rules, and one draw needn't show every extreme that they name: `buckets`: each of the values 0, 1, 2 is taken by exactly 16 blocks. For block b with 2**buckets[b] rows, slots j < 2**buckets[b] hold lengths of 1 to 512 / 2**buckets[b], slot 0 always the full row size; the other slots are 0.
All inputs are finite; a program needn't handle non-finite values.
Results may differ from a plain program's by a relative error of at most 0.018.
Values may be sent and summed in bfloat16 or wider, within the bound.
A program may use at most 128 MiB of HBM per device.

v0:
```python
import jax
import jax.numpy as jnp
from jax import lax
from jax.sharding import PartitionSpec as P

HEAD_DIM = 64
SEG = 512


NEG = -1e30
EPS = 1e-12
INV_ROOT_TWO = 0.7071067811865476
INV_ROOT_TWO_PI = 0.3989422804014327


def block_layout(bucket, lens):
    places = jnp.arange(SEG, dtype=jnp.int32)
    span = jnp.where(bucket == 0, SEG, jnp.where(bucket == 1, SEG // 2, SEG // 4)).astype(jnp.int32)
    row_ids = places // span
    inside = places - row_ids * span
    slots = jnp.arange(4, dtype=jnp.int32)
    row_len = jnp.sum(jnp.where(row_ids[:, None] == slots[None, :], lens[None, :], 0), axis=1)
    return (row_ids, inside < row_len)


def whole_mask(bucket, lens):
    row_ids, valid = block_layout(bucket, lens)
    return ((row_ids[:, None] == row_ids[None, :]) & valid[None, :])[None]


def score_block(query, keys, allowed, groups):
    span = SEG // groups
    heads = query.shape[1]
    query_g = query.reshape(groups, span, heads, HEAD_DIM)
    keys_g = keys.reshape(groups, span, heads, HEAD_DIM)
    scores = jnp.einsum(
        "gqhe,gkhe->ghqk", query_g, keys_g, preferred_element_type=jnp.float32
    ) * HEAD_DIM ** (-0.5)
    return (jnp.where(allowed[:, None], scores, NEG), query_g, keys_g)


def attend_forward(query, keys, values, allowed, groups):
    span = SEG // groups
    heads = query.shape[1]
    scores, query_g, keys_g = score_block(query, keys, allowed, groups)
    top = jnp.max(scores, axis=-1, keepdims=True)
    totals = top + jnp.log(jnp.sum(jnp.exp(scores - top), axis=-1, keepdims=True))
    probs = jnp.exp(scores - totals).astype(jnp.bfloat16)
    values_g = values.reshape(groups, span, heads, HEAD_DIM)
    context = jnp.einsum("ghqk,gkhe->gqhe", probs, values_g, preferred_element_type=jnp.float32)
    context = context.reshape(SEG, heads * HEAD_DIM).astype(jnp.bfloat16)
    return (context, totals[..., 0].transpose(0, 2, 1).reshape(SEG, heads))


def attend_backward(query, keys, values, context_grad, totals, allowed, groups):
    span = SEG // groups
    heads = query.shape[1]
    scores, query_g, keys_g = score_block(query, keys, allowed, groups)
    totals_g = totals.reshape(groups, span, heads).transpose(0, 2, 1)[..., None]
    probs = jnp.exp(scores - totals_g)
    values_g = values.reshape(groups, span, heads, HEAD_DIM)
    grad_g = context_grad.reshape(groups, span, heads, HEAD_DIM)
    prob_grad = jnp.einsum("gqhe,gkhe->ghqk", grad_g, values_g, preferred_element_type=jnp.float32)
    values_grad = jnp.einsum(
        "ghqk,gqhe->gkhe", probs.astype(jnp.bfloat16), grad_g, preferred_element_type=jnp.float32
    )
    score_grad = (probs * (prob_grad - jnp.sum(probs * prob_grad, axis=-1, keepdims=True))).astype(
        jnp.bfloat16
    )
    query_grad = jnp.einsum(
        "ghqk,gkhe->gqhe", score_grad, keys_g, preferred_element_type=jnp.float32
    ) * HEAD_DIM ** (-0.5)
    keys_grad = jnp.einsum(
        "ghqk,gqhe->gkhe", score_grad, query_g, preferred_element_type=jnp.float32
    ) * HEAD_DIM ** (-0.5)
    width = heads * HEAD_DIM
    return (
        query_grad.reshape(SEG, width).astype(jnp.bfloat16),
        keys_grad.reshape(SEG, width).astype(jnp.bfloat16),
        values_grad.reshape(SEG, width).astype(jnp.bfloat16),
    )


def block_forward(item):
    query, keys, values, bucket, lens = item
    return attend_forward(query, keys, values, whole_mask(bucket, lens), 1)


def block_backward(item):
    query, keys, values, context_grad, totals, bucket, lens = item
    return attend_backward(query, keys, values, context_grad, totals, whole_mask(bucket, lens), 1)


def norm_forward(value):
    centre = value - jnp.mean(value, axis=-1, keepdims=True)
    inverse = lax.rsqrt(jnp.mean(centre * centre, axis=-1, keepdims=True) + EPS)
    return (centre * inverse, inverse)


def norm_backward(upstream, normed, inverse, gain):
    scaled = upstream * gain
    return inverse * (
        scaled
        - jnp.mean(scaled, axis=-1, keepdims=True)
        - normed * jnp.mean(scaled * normed, axis=-1, keepdims=True)
    )


def gelu_slope(inner):
    return (
        0.5 * (1.0 + jax.scipy.special.erf(inner * INV_ROOT_TWO))
        + inner * jnp.exp(-0.5 * inner * inner) * INV_ROOT_TWO_PI
    )


def forward_pass(
    tokens,
    lengths,
    buckets,
    w_query,
    b_query,
    w_key,
    w_value,
    b_value,
    w_out,
    b_out,
    norm1_gain,
    norm1_bias,
    w_up,
    b_up,
    w_down,
    b_down,
):
    blocks = buckets.shape[0]
    width = w_query.shape[1]
    heads = width // HEAD_DIM
    gathered = lax.all_gather(tokens, "mp", axis=0, tiled=True)
    query = (
        jnp.dot(gathered, w_query, preferred_element_type=jnp.float32) + b_query.astype(jnp.float32)
    ).astype(jnp.bfloat16)
    keys = jnp.dot(gathered, w_key, preferred_element_type=jnp.float32).astype(jnp.bfloat16)
    values = (
        jnp.dot(gathered, w_value, preferred_element_type=jnp.float32) + b_value.astype(jnp.float32)
    ).astype(jnp.bfloat16)
    shape = (blocks, SEG, heads, HEAD_DIM)
    query_b = query.reshape(shape)
    keys_b = keys.reshape(shape)
    values_b = values.reshape(shape)
    context, totals = lax.map(block_forward, (query_b, keys_b, values_b, buckets, lengths))
    context = context.reshape(blocks * SEG, width)
    attended = lax.psum_scatter(
        jnp.dot(context, w_out, preferred_element_type=jnp.float32).astype(jnp.bfloat16),
        "mp",
        scatter_dimension=0,
        tiled=True,
    ).astype(jnp.float32)
    normed1, inverse1 = norm_forward(
        tokens.astype(jnp.float32) + attended + b_out.astype(jnp.float32)
    )
    hidden = (normed1 * norm1_gain.astype(jnp.float32) + norm1_bias.astype(jnp.float32)).astype(
        jnp.bfloat16
    )
    hidden_rows = lax.all_gather(hidden, "mp", axis=0, tiled=True)
    inner = jnp.dot(hidden_rows, w_up, preferred_element_type=jnp.float32) + b_up.astype(
        jnp.float32
    )
    active = jax.nn.gelu(inner, approximate=False).astype(jnp.bfloat16)
    branch = lax.psum_scatter(
        jnp.dot(active, w_down, preferred_element_type=jnp.float32).astype(jnp.bfloat16),
        "mp",
        scatter_dimension=0,
        tiled=True,
    ).astype(jnp.float32)
    normed2, inverse2 = norm_forward(
        hidden.astype(jnp.float32) + branch + b_down.astype(jnp.float32)
    )
    return (
        gathered,
        query_b,
        keys_b,
        values_b,
        context,
        totals,
        normed1,
        inverse1,
        hidden_rows,
        inner,
        active,
        normed2,
        inverse2,
    )


def shards(
    tokens,
    lengths,
    buckets,
    w_query,
    b_query,
    w_key,
    w_value,
    b_value,
    w_out,
    b_out,
    norm1_gain,
    norm1_bias,
    w_up,
    b_up,
    w_down,
    b_down,
    norm2_gain,
    norm2_bias,
    cotangent,
):
    half = tokens.shape[0]
    blocks = buckets.shape[0]
    width = w_query.shape[1]
    weights = (
        w_query,
        b_query,
        w_key,
        w_value,
        b_value,
        w_out,
        b_out,
        norm1_gain,
        norm1_bias,
        w_up,
        b_up,
        w_down,
        b_down,
    )
    state = forward_pass(tokens, lengths, buckets, *weights)
    normed2 = state[11]
    gain1 = norm1_gain.astype(jnp.float32)
    gain2 = norm2_gain.astype(jnp.float32)
    valid_all = jax.vmap(block_layout)(buckets, lengths)[1].reshape(blocks * SEG)
    keep = lax.dynamic_slice_in_dim(valid_all, lax.axis_index("mp") * half, half).astype(
        jnp.float32
    )[:, None]
    output = ((normed2 * gain2 + norm2_bias.astype(jnp.float32)) * keep).astype(jnp.bfloat16)
    (
        gathered,
        query_b,
        keys_b,
        values_b,
        context,
        totals,
        normed1,
        inverse1,
        hidden_rows,
        inner,
        active,
        normed2,
        inverse2,
    ) = state
    upstream = cotangent.astype(jnp.float32) * keep
    norm2_gain_grad = jnp.sum(upstream * normed2, axis=0)
    norm2_bias_grad = jnp.sum(upstream, axis=0)
    second_grad = norm_backward(upstream, normed2, inverse2, gain2)
    b_down_grad = jnp.sum(second_grad, axis=0)
    branch_grad = lax.all_gather(second_grad.astype(jnp.bfloat16), "mp", axis=0, tiled=True)
    w_down_grad = jnp.einsum("tf,td->fd", active, branch_grad, preferred_element_type=jnp.float32)
    active_grad = jnp.einsum("td,fd->tf", branch_grad, w_down, preferred_element_type=jnp.float32)
    inner_grad = (active_grad * gelu_slope(inner)).astype(jnp.bfloat16)
    b_up_grad = jnp.sum(inner_grad.astype(jnp.float32), axis=0)
    w_up_grad = jnp.einsum("td,tf->df", hidden_rows, inner_grad, preferred_element_type=jnp.float32)
    hidden_grad = (
        lax.psum_scatter(
            jnp.einsum("tf,df->td", inner_grad, w_up, preferred_element_type=jnp.float32).astype(
                jnp.bfloat16
            ),
            "mp",
            scatter_dimension=0,
            tiled=True,
        ).astype(jnp.float32)
        + second_grad
    )
    norm1_gain_grad = jnp.sum(hidden_grad * normed1, axis=0)
    norm1_bias_grad = jnp.sum(hidden_grad, axis=0)
    first_grad = norm_backward(hidden_grad, normed1, inverse1, gain1)
    b_out_grad = jnp.sum(first_grad, axis=0)
    attn_grad = lax.all_gather(first_grad.astype(jnp.bfloat16), "mp", axis=0, tiled=True)
    w_out_grad = jnp.einsum("tc,td->cd", context, attn_grad, preferred_element_type=jnp.float32)
    context_grad = jnp.einsum(
        "td,cd->tc", attn_grad, w_out, preferred_element_type=jnp.float32
    ).astype(jnp.bfloat16)
    query_grad, keys_grad, values_grad = lax.map(
        block_backward,
        (
            query_b,
            keys_b,
            values_b,
            context_grad.reshape(blocks, SEG, width),
            totals,
            buckets,
            lengths,
        ),
    )
    query_grad = query_grad.reshape(blocks * SEG, width)
    keys_grad = keys_grad.reshape(blocks * SEG, width)
    values_grad = values_grad.reshape(blocks * SEG, width)
    w_query_grad = jnp.einsum("td,tc->dc", gathered, query_grad, preferred_element_type=jnp.float32)
    w_key_grad = jnp.einsum("td,tc->dc", gathered, keys_grad, preferred_element_type=jnp.float32)
    w_value_grad = jnp.einsum(
        "td,tc->dc", gathered, values_grad, preferred_element_type=jnp.float32
    )
    b_query_grad = jnp.sum(query_grad.astype(jnp.float32), axis=0)
    b_value_grad = jnp.sum(values_grad.astype(jnp.float32), axis=0)
    total = jnp.einsum("tc,dc->td", query_grad, w_query, preferred_element_type=jnp.float32)
    total = total + jnp.einsum("tc,dc->td", keys_grad, w_key, preferred_element_type=jnp.float32)
    input_grad = (
        lax.psum_scatter(
            (
                total
                + jnp.einsum("tc,dc->td", values_grad, w_value, preferred_element_type=jnp.float32)
            ).astype(jnp.bfloat16),
            "mp",
            scatter_dimension=0,
            tiled=True,
        ).astype(jnp.float32)
        + first_grad
    )
    vectors = lax.psum(
        (
            b_out_grad,
            norm1_gain_grad,
            norm1_bias_grad,
            b_down_grad,
            norm2_gain_grad,
            norm2_bias_grad,
        ),
        ("dp", "mp"),
    )
    summed = lax.psum(
        (
            w_query_grad,
            b_query_grad,
            w_key_grad,
            w_value_grad,
            b_value_grad,
            w_out_grad,
            w_up_grad,
            b_up_grad,
            w_down_grad,
        ),
        "dp",
    )
    return (
        output,
        input_grad,
        summed[0],
        summed[1],
        summed[2],
        summed[3],
        summed[4],
        summed[5],
        vectors[0],
        vectors[1],
        vectors[2],
        summed[6],
        summed[7],
        summed[8],
        vectors[3],
        vectors[4],
        vectors[5],
    )


def solution(mesh):
    placed = (
        P(("dp", "mp"), None),
        P("dp", None),
        P("dp"),
        P(None, "mp"),
        P("mp"),
        P(None, "mp"),
        P(None, "mp"),
        P("mp"),
        P("mp", None),
        P(),
        P(),
        P(),
        P(None, "mp"),
        P("mp"),
        P("mp", None),
        P(),
        P(),
        P(),
        P(("dp", "mp"), None),
    )
    return jax.shard_map(
        shards,
        mesh=mesh,
        in_specs=placed,
        out_specs=(
            P(("dp", "mp"), None),
            P(("dp", "mp"), None),
            P(None, "mp"),
            P("mp"),
            P(None, "mp"),
            P(None, "mp"),
            P("mp"),
            P("mp", None),
            P(),
            P(),
            P(),
            P(None, "mp"),
            P("mp"),
            P("mp", None),
            P(),
            P(),
            P(),
        ),
        check_vma=False,
    )
```

profile of v0, /device:TPU:1, one launch (start us, length us, event | category | flops | bytes accessed | tf_op | source)
XLA Modules:
  0.0 818.7 jit_solution(2867742267802248285)
XLA Ops:
  9.4 38.4 %all-gather.5.cloned.1.call-done = bf16[1536,768]{1,0:T(8,128)(2,1)} async-done(((bf16[768,768]{1,0:T(8,128)(2,1)}), bf16[1536,768]{1,0:T(8,128)(2,1)}) %all-gather.5.cloned.1.call-update) | async-done | bytes 2359312 | tf_op jit(solution)/shard_map/all_gather | solution.py:137
  47.8 3.2 convolution_convert_fusion.4
  50.9 3.1 reshape.616
  54.0 3.5 copy.80
  57.5 4.2 fusion.62
  61.7 4.7 reshape.615
  66.4 4.4 copy.79
  70.8 4.2 fusion.61
  75.0 4.7 reshape.614
  79.6 4.4 copy.78
  85.2 43.5 %while.30 = (s32[]{:T(128)}, bf16[3,512,384]{2,1,0:T(8,128)(2,1)}, f32[3,512,6]{1,2,0:T(8,128)}, bf16[3,512,6,64]{1,3,2,0:T(8,128)(2,1)}, s32[3]{0:T(128)S(1)}, ...) while((s32[]{:T(128)}, bf16[3,512,384]{2,1,0:T(8,128)(2,1)}, ...), condition=%wide.region_4.5_spmd, body=%wide.region_0.4_spmd.sunk | while | flops 420687872 | bytes 23183644 | solution.py:149
  88.3 2.2 fusion.143
  92.5 3.5 fusion.144
  102.8 2.2 fusion.143
  107.0 3.5 fusion.144
  117.4 2.2 fusion.143
  121.5 3.5 fusion.144
  129.7 4.2 convolution_convert_fusion.2
  135.9 32.9 %reduce-scatter.5.cloned.1.call-done = bf16[768,768]{1,0:T(8,128)(2,1)} async-done(((bf16[1536,768]{1,0:T(8,128)(2,1)}), bf16[768,768]{1,0:T(8,128)(2,1)}) %reduce-scatter.5.cloned.1.call-update) | async-done | bytes 1179664 | tf_op jit(solution)/shard_map/reduce_scatter | solution.py:151
  174.5 34.9 %all-gather.7.cloned.1.call-done = bf16[1536,768]{1,0:T(8,128)(2,1)} async-done(((bf16[768,768]{1,0:T(8,128)(2,1)}), bf16[1536,768]{1,0:T(8,128)(2,1)}) %all-gather.7.cloned.1.call-update) | async-done | bytes 2359312 | tf_op jit(solution)/shard_map/all_gather | solution.py:163
  209.3 25.4 %fusion.48 = (bf16[1536,1536]{1,0:T(8,128)(2,1)S(1)}, f32[1536,1536]{1,0:T(8,128)}) fusion(f32[1536]{0:T(1024)} %convert_element_type.227, bf16[1536,768]{1,0:T(8,128)(2,1)} %all-gather.7.cloned.1.call-done, bf16[768,1536]{1,0:T(8,128)(2,1)S(1)} %copy-done), kind=kOutput, calls=%fused_computation.80 | convolution fusion | flops 3779592192 | bytes 18880512 | tf_op jit(solution)/shard_map/dot_general | solution.py:164
  234.8 2.2 copy-done.45
  236.9 5.0 convolution_convert_fusion.1
  257.6 19.3 %reduce-scatter.7.cloned.1.call-done = bf16[768,768]{1,0:T(8,128)(2,1)} async-done(((bf16[1536,768]{1,0:T(8,128)(2,1)}), bf16[768,768]{1,0:T(8,128)(2,1)}) %reduce-scatter.7.cloned.1.call-update) | async-done | bytes 1179664 | tf_op jit(solution)/shard_map/reduce_scatter | solution.py:168
  276.8 2.2 fusion.67
  279.9 2.3 multiply_reduce_fusion.1
  282.2 2.9 fusion.76
  285.2 36.2 %all-gather.9.cloned.1.call-done = bf16[1536,768]{1,0:T(8,128)(2,1)} async-done(((bf16[768,768]{1,0:T(8,128)(2,1)}), bf16[1536,768]{1,0:T(8,128)(2,1)}) %all-gather.9.cloned.1.call-update) | async-done | bytes 2359312 | tf_op jit(solution)/shard_map/all_gather | solution.py:262
  321.4 10.8 %convert_reduce_fusion = (f32[1536]{0:T(1024)}, bf16[1536,1536]{1,0:T(8,128)(2,1)S(1)}) fusion(f32[1536,1536]{1,0:T(8,128)} %get-tuple-element.451, bf16[1536,768]{1,0:T(8,128)(2,1)} %all-gather.9.cloned.1.call-done, bf16[1536,768]{1,0:T(8,128)(2,1)} %param.37), kind=kOutput, calls=%fused_computation.85 | convolution fusion | flops 3652188672 | bytes 18880512 | tf_op jit(solution)/shard_map/td,fd->tf/dot_general | solution.py:264
  332.2 2.2 copy-done.44
  334.4 5.1 convolution_convert_fusion
  339.5 34.8 %reduce-scatter.9.cloned.1.call-done = bf16[768,768]{1,0:T(8,128)(2,1)} async-done(((bf16[1536,768]{1,0:T(8,128)(2,1)}), bf16[768,768]{1,0:T(8,128)(2,1)}) %reduce-scatter.9.cloned.1.call-update) | async-done | bytes 1179664 | tf_op jit(solution)/shard_map/reduce_scatter | solution.py:269
  374.4 3.9 multiply_reduce_fusion.2
  383.1 36.0 %all-gather.11.cloned.1.call-done = bf16[1536,768]{1,0:T(8,128)(2,1)} async-done(((bf16[768,768]{1,0:T(8,128)(2,1)}), bf16[1536,768]{1,0:T(8,128)(2,1)}) %all-gather.11.cloned.1.call-update) | async-done | bytes 2359312 | tf_op jit(solution)/shard_map/all_gather | solution.py:283
  419.0 4.1 convolution_convert_fusion.3
  424.4 58.7 %while.31 = (s32[]{:T(128)}, bf16[3,512,384]{1,2,0:T(8,128)(2,1)}, bf16[3,512,384]{2,1,0:T(8,128)(2,1)}, bf16[3,512,384]{1,2,0:T(8,128)(2,1)}, bf16[3,512,6,64]{...) while((s32[]{:T(128)}, bf16[3,512,384]{1,2,0:T(8,128)(2,1)}, ...), condition=%wide.region_20.21_spmd, body=%wide.region_17.20_spmd.sunk | while | flops 1031745536 | bytes 58556768 | solution.py:288
  429.5 2.0 fusion.154
  431.5 2.5 fusion.156
  434.1 3.2 multiply_reduce_fusion.9
  439.2 2.1 fusion.158
  449.1 2.0 fusion.154
  451.1 2.5 fusion.156
  453.6 3.2 multiply_reduce_fusion.9
  458.8 2.1 fusion.158
  468.6 2.0 fusion.154
  470.7 2.5 fusion.156
  473.2 3.2 multiply_reduce_fusion.9
  476.4 1.9 multiply_convert_fusion.3
  478.4 2.1 fusion.158
  486.8 2.5 fusion.79
  490.8 3.0 add_convert_fusion
  493.9 9.3 %fusion.82 = f32[1536,768]{1,0:T(8,128)} fusion(bf16[1536,1536]{1,0:T(8,128)(2,1)} %copy-done.45, bf16[1536,768]{1,0:T(8,128)(2,1)} %all-gather.9.cloned.1.call-done), kind=kOutput, calls=%fused_computation.173 | convolution fusion | flops 3623878656 | bytes 11796480 | tf_op jit(solution)/shard_map/tf,td->fd/dot_general | solution.py:263
  503.2 8.2 %fusion.81 = f32[768,1536]{1,0:T(8,128)} fusion(bf16[1536,768]{1,0:T(8,128)(2,1)S(1)} %copy-done.39, bf16[1536,1536]{1,0:T(8,128)(2,1)} %copy-done.44), kind=kOutput, calls=%fused_computation.172 | convolution fusion | flops 3623878656 | bytes 11796480 | tf_op jit(solution)/shard_map/td,tf->df/dot_general | solution.py:267
  511.4 2.1 fusion.80
  513.6 2.1 convolution_bitcast_fusion.2
  515.7 2.1 convolution_bitcast_fusion
  517.8 2.1 convolution_bitcast_fusion.1
  520.7 41.3 %all-reduce = (f32[768]{0:T(1024)}, f32[768]{0:T(1024)}, f32[768]{0:T(1024)}, f32[768]{0:T(1024)}, f32[768]{0:T(1024)}, /*index=5*/f32[768]{0:T(1024)}) all-reduce(f32[768]{0:T(1024)S(1)} %copy-done.31, f32[768]{0:T(1024)S(1)} %copy-done.28, f32[768]{0:T(1024)S(1)} %copy-done.29, ...), channel_id=1, replica_groups=mesh['dp'=16,'mp'=2] {'dp','mp'}, use_global_device_ids=true, to_apply=%region_31.32 | all-reduce | flops 4608 | bytes 36864 | tf_op jit(solution)/shard_map/psum | solution.py:324
  563.8 59.3 %all-reduce.1 = (f32[384]{0:T(512)}, f32[384]{0:T(512)}, f32[1536]{0:T(1024)}) all-reduce(f32[384]{0:T(512)S(1)} %convert_reduce_fusion.2, f32[384]{0:T(512)S(1)} %convert_reduce_fusion.1, f32[1536]{0:T(1024)S(1)} %copy-done.33), channel_id=1, replica_groups=mesh['dp'=16,'mp'=2] {'dp'}, use_global_device_ids=true, to_apply=%region_24.25 | all-reduce | flops 2304 | bytes 18432 | tf_op jit(solution)/shard_map/psum | solution.py:335
  623.1 2.9 convert_add_fusion
  626.0 170.2 %all-reduce.5.cloned.1.call-done = (f32[768,384]{0,1:T(8,128)}, f32[768,384]{0,1:T(8,128)}, f32[768,384]{0,1:T(8,128)}, f32[384,768]{1,0:T(8,128)}, f32[768,1536]{1,0:T(8,128)}, /*index=5*/f32[1536,768]{1,0:T(8,128)}) async-done(((f32[768,384]{0,1:T(8,128)}, f32[768,384]{0,1:T(8,128)}, f32[768,384]{0,1:T(8,128)}, f32[384,768]{1,0:T(8,128)}, f32[768,1536]{1,0:T(8,128)}, /*index=5*/f32[1536,768]{1,0:T(8,128)}), ...) | async-done | bytes 14155792 | tf_op jit(solution)/shard_map/psum | solution.py:335
  796.2 2.8 copy.89
  802.8 5.5 copy.148
  808.3 2.4 copy.149
  (236 shorter events, 92.2 us)
Async XLA Ops:
  7.2 202.2 %copy-start = (bf16[768,1536]{1,0:T(8,128)(2,1)S(1)}, bf16[768,1536]{1,0:T(8,128)(2,1)}, u32[]{:S(2)}) copy-start(bf16[768,1536]{1,0:T(8,128)(2,1)} %param.35) | copy-start | bytes 7077892
  7.2 40.6 %all-gather.5.cloned.1.call-start = ((), (), s32[]{:S(2)}) async-start(), calls=%async_computation.4 | async-start | bytes 3538944 | tf_op jit(solution)/shard_map/all_gather | solution.py:137
  7.9 160.9 %reduce-scatter.5.cloned.1.call-start = ((), (), s32[]{:S(2)}) async-start(), calls=%async_computation.5 | async-start | bytes 3538944 | tf_op jit(solution)/shard_map/reduce_scatter | solution.py:151
  79.6 5.5 copy-start.42
  128.7 1.0 copy-start.4
  133.9 0.7 copy-start.34
  133.9 0.7 copy-start.35
  133.9 34.9 %copy-start.2 = (bf16[768,768]{1,0:T(8,128)(2,1)S(1)}, bf16[768,768]{1,0:T(8,128)(2,1)}, u32[]{:S(2)}) copy-start(bf16[768,768]{1,0:T(8,128)(2,1)} %param.23) | copy-start | bytes 3538948
  134.0 75.4 %all-gather.7.cloned.1.call-start = ((), (), s32[]{:S(2)}) async-start(), calls=%async_computation.6 | async-start | bytes 3538944 | tf_op jit(solution)/shard_map/all_gather | solution.py:163
  168.8 1.8 copy-start.6
  168.8 2.5 copy-start.32
  171.4 1.7 copy-start.23
  173.1 103.7 %reduce-scatter.7.cloned.1.call-start = ((), (), s32[]{:S(2)}) async-start(), calls=%async_computation.7 | async-start | bytes 3538944 | tf_op jit(solution)/shard_map/reduce_scatter | solution.py:168
  209.3 27.6 %copy-start.37 = (bf16[1536,768]{1,0:T(8,128)(2,1)S(1)}, bf16[1536,768]{1,0:T(8,128)(2,1)}, u32[]{:S(2)}) copy-start(bf16[1536,768]{1,0:T(8,128)(2,1)} %param.37) | copy-start | bytes 7077892
  234.7 2.2 copy-start.45
  242.0 79.4 %all-gather.9.cloned.1.call-start = ((), (), s32[]{:S(2)}) async-start(), calls=%async_computation.8 | async-start | bytes 3538944 | tf_op jit(solution)/shard_map/all_gather | solution.py:262
  245.9 0.8 copy-start.36
  276.8 2.3 copy-start.3
  276.8 2.3 copy-start.11
  276.8 3.0 copy-start.16
  276.8 3.0 copy-start.25
  276.8 3.0 copy-start.26
  279.8 2.4 copy-start.27
  285.2 89.2 %reduce-scatter.9.cloned.1.call-start = ((), (), s32[]{:S(2)}) async-start(), calls=%async_computation.9 | async-start | bytes 3538944 | tf_op jit(solution)/shard_map/reduce_scatter | solution.py:269
  332.2 2.2 copy-start.44
  339.5 34.9 %copy-start.7 = (bf16[768,768]{1,0:T(8,128)(2,1)S(1)}, bf16[768,768]{1,0:T(8,128)(2,1)}, u32[]{:S(2)}) copy-start(bf16[768,768]{1,0:T(8,128)(2,1)} %reduce-scatter.5.cloned.1.call-done) | copy-start | bytes 3538948
  339.5 34.9 %copy-start.24 = (f32[768]{0:T(1024)S(1)}, f32[768]{0:T(1024)}, u32[]{:S(2)}) copy-start(f32[768]{0:T(1024)} %copy-done.23) | copy-start | bytes 9220
  339.5 79.5 %all-gather.11.cloned.1.call-start = ((), (), s32[]{:S(2)}) async-start(), calls=%async_computation.10 | async-start | bytes 3538944 | tf_op jit(solution)/shard_map/all_gather | solution.py:283
  374.4 3.9 copy-start.10
  374.4 3.9 copy-start.14
  380.2 1.4 copy-start.8
  381.6 37.4 %copy-start.41 = (bf16[384,768]{1,0:T(8,128)(2,1)S(1)}, bf16[384,768]{1,0:T(8,128)(2,1)}, u32[]{:S(2)}) copy-start(bf16[384,768]{1,0:T(8,128)(2,1)} %param.31) | copy-start | bytes 1769476
  382.8 240.3 %reduce-scatter.11.cloned.1.call-start = ((), (), s32[]{:S(2)}) async-start(), calls=%async_computation.11 | async-start | bytes 3538944 | tf_op jit(solution)/shard_map/reduce_scatter | solution.py:313
  383.0 41.3 %copy-start.5 = (bf16[3,512,6,64]{1,3,2,0:T(8,128)(2,1)S(1)}, bf16[3,512,6,64]{1,3,2,0:T(8,128)(2,1)}, u32[]{:S(2)}) copy-start(bf16[3,512,6,64]{1,3,2,0:T(8,128)(2,1)} %copy-done.4) | copy-start | bytes 3538948
  383.1 41.3 %copy-start.43 = (s32[3]{0:T(128)S(1)}, s32[3]{0:T(128)}, u32[]{:S(2)}) copy-start(s32[3]{0:T(128)} %param.25) | copy-start | bytes 40
  441.3 1.7 copy-start.12
  460.9 1.7 copy-start.12
  480.5 1.7 copy-start.12
  483.1 3.7 copy-start.13
  486.8 2.6 copy-start.21
  489.4 1.4 copy-start.22
  493.8 302.4 %all-reduce.5.cloned.1.call-start = ((), (), s32[]{:S(2)}) async-start(), calls=%async_computation.12 | async-start | bytes 28311552 | tf_op jit(solution)/shard_map/psum | solution.py:335
  493.9 9.3 %copy-start.39 = (bf16[1536,768]{1,0:T(8,128)(2,1)S(1)}, bf16[1536,768]{1,0:T(8,128)(2,1)}, u32[]{:S(2)}) copy-start(bf16[1536,768]{1,0:T(8,128)(2,1)} %all-gather.7.cloned.1.call-done) | copy-start | bytes 7077892
  503.2 8.2 %copy-start.20 = (bf16[3,512,384]{2,1,0:T(8,128)(2,1)S(1)}, bf16[3,512,384]{2,1,0:T(8,128)(2,1)}, u32[]{:S(2)}) copy-start(bf16[3,512,384]{2,1,0:T(8,128)(2,1)} %get-tuple-element.258) | copy-start | bytes 3538948
  503.2 8.2 %copy-start.40 = (bf16[1536,768]{1,0:T(8,128)(2,1)S(1)}, bf16[1536,768]{1,0:T(8,128)(2,1)}, u32[]{:S(2)}) copy-start(bf16[1536,768]{1,0:T(8,128)(2,1)} %all-gather.11.cloned.1.call-done) | copy-start | bytes 7077892
  511.4 2.1 copy-start.38
  519.9 0.7 copy-start.28
  519.9 0.7 copy-start.29
  520.0 0.7 copy-start.30
  520.0 0.7 copy-start.31
  520.0 42.0 %copy-start.15 = (bf16[3,512,384]{1,2,0:T(8,128)(2,1)S(1)}, bf16[3,512,384]{1,2,0:T(8,128)(2,1)}, u32[]{:S(2)}) copy-start(bf16[3,512,384]{1,2,0:T(8,128)(2,1)} %get-tuple-element.262) | copy-start | bytes 3538948
  520.0 103.1 %copy-start.9 = (f32[768,768]{1,0:T(8,128)S(1)}, f32[768,768]{1,0:T(8,128)}, u32[]{:S(2)}) copy-start(f32[768,768]{1,0:T(8,128)} %copy-done.8) | copy-start | bytes 7077892
  562.0 1.8 copy-start.33
  796.2 2.8 copy-start.19
  796.2 4.2 copy-start.18
  799.0 2.8 copy-start.17
  801.8 6.5 slice-start
  802.8 5.5 slice-start.1
  808.3 3.4 copy-start.1
Sparse Core Ops, SparseCore 0:
  9.6 38.1 all-gather.4
  134.1 34.7 reduce-scatter.4
  173.2 36.0 all-gather.6
  242.1 34.6 reduce-scatter.6
  285.3 36.0 all-gather.8
  339.6 34.7 reduce-scatter.8
  382.9 36.0 all-gather.10
  494.0 34.6 reduce-scatter.10
  535.0 261.1 all-reduce.4
where the time goes:
time: 832 us; the launch traced here: 819 us
  waiting for transfers between devices  403 us (48%)
  matrix products  148 us (18%)
  blocking collectives  101 us (12%)
  local copies, waits for them, and re-layouts  91.8 us (11%)
  other arithmetic  51.5 us (6%)
  between operations  14.6 us (2%)
    psum x1, waiting for transfers between devices, shards(): lax.psum((w_query_grad, b_query_grad, w_key_grad, w_value_grad, b_value_g...  170 us
    psum x1, blocking collectives, shards(): lax.psum((w_query_grad, b_query_grad, w_key_grad, w_value_grad, b_value_g...  59.3 us
    psum x1, blocking collectives, shards(): lax.psum((b_out_grad, norm1_gain_grad, norm1_bias_grad, b_down_grad, norm...  41.3 us
    all_gather x1, waiting for transfers between devices, forward_pass(): gathered = lax.all_gather(tokens, 'mp', axis=0, tiled=True)  38.4 us
    all_gather x1, waiting for transfers between devices, shards(): lax.all_gather(second_grad.astype(jnp.bfloat16), 'mp', axis=0, tiled=True)  36.2 us
    all_gather x1, waiting for transfers between devices, shards(): lax.all_gather(first_grad.astype(jnp.bfloat16), 'mp', axis=0, tiled=True)  36 us
    all_gather x1, waiting for transfers between devices, forward_pass(): hidden_rows = lax.all_gather(hidden, 'mp', axis=0, tiled=True)  34.9 us
    reduce_scatter x1, waiting for transfers between devices, shards(): lax.psum_scatter(jnp.einsum('tf,df->td', inner_grad, w_up, preferred_elem...  34.8 us
  transfers between devices with their start and end apart: 9, of which 8 were waited for; matrix products, arithmetic and copies ran while one was open for 6% of the time, Pallas kernels for 0%

commit v1 on v0

v1 whole, which is shorter than its diff:
```python
import functools

import jax
import jax.numpy as jnp
from jax import lax
from jax.experimental import pallas as pl
from jax.experimental.pallas import tpu as pltpu
from jax.sharding import Mesh, PartitionSpec as P

HEAD_DIM = 64
SEG = 512
PAIR = 2 * HEAD_DIM
NEG = -1e30
EPS = 1e-12
ROOT_HALF = 0.7071067811865476
INV_ROOT_TWO_PI = 0.3989422804014327
F32 = jnp.float32
BF16 = jnp.bfloat16
VMEM_LIMIT = 60 * 1024 * 1024
TILE = 256
FFN_PARTS = 4
ATT_PARTS = 2


def mm(left, right):
    return lax.dot_general(left, right, (((1,), (0,)), ((), ())), preferred_element_type=F32)


def mm_nt(left, right):
    return lax.dot_general(left, right, (((1,), (1,)), ((), ())), preferred_element_type=F32)


def call(body, grid, pos, inputs, in_specs, out_shape, out_specs, scratch, flops, name):
    moved = sum(v.size * v.dtype.itemsize for v in inputs) + sum(
        v.size * v.dtype.itemsize for v in out_shape
    )
    return pl.pallas_call(
        body,
        grid_spec=pltpu.PrefetchScalarGridSpec(
            num_scalar_prefetch=1,
            grid=grid,
            in_specs=in_specs,
            out_specs=out_specs,
            scratch_shapes=scratch,
        ),
        out_shape=out_shape,
        compiler_params=pltpu.CompilerParams(
            dimension_semantics=("arbitrary",) * len(grid), vmem_limit_bytes=VMEM_LIMIT
        ),
        cost_estimate=pl.CostEstimate(flops=flops, bytes_accessed=moved, transcendentals=0),
        name=name,
    )(pos, *inputs)


def whole(array):
    zeros = (0,) * array.ndim
    return pl.BlockSpec(array.shape, lambda j, pos: zeros)


def shape(dims, kind):
    return jax.ShapeDtypeStruct(dims, kind)


def gelu_parts(inner):
    erf = lax.erf(inner * ROOT_HALF)
    below = 0.5 + 0.5 * erf
    density = jnp.exp(inner * inner * -0.5) * INV_ROOT_TWO_PI
    return inner * below, below + inner * density


def attend_forward_body(gathered, pos_ref, x_ref, *refs):
    if gathered:
        (p0, p1, pc, bq, bv, qs_a, ks_a, qs_m, ks_m) = refs[:9]
        (q_o, k_o, v_o, ctx_o, pa_o, pm_o, w_o, mask_a, mask_m, w_s) = refs[9:]
    else:
        (wq, wk, wv, bq, bv, qs_a, ks_a, qs_m, ks_m) = refs[:9]
        (q_o, k_o, v_o, ctx_o, pa_o, pm_o, mask_a, mask_m) = refs[9:]
    j = pl.program_id(0)
    rows = q_o.shape[0]
    half = rows - SEG

    @pl.when(j == 0)
    def _():
        mask_a[...] = jnp.where(ks_a[...] == qs_a[...], 0.0, NEG)
        mask_m[...] = jnp.where(ks_m[...] == qs_m[...], 0.0, NEG)
        if gathered:
            quarter = p0.shape[0]
            width = p0.shape[1] // 3
            for rel, piece in enumerate((p0, p1, pc.at[0], pc.at[1])):
                row = pl.multiple_of((pos_ref[0] ^ rel) * quarter, 16)
                for pair in range(width // PAIR):
                    for part in range(3):
                        w_s[pair, pl.ds(row, quarter), part * PAIR : (part + 1) * PAIR] = piece[
                            :, part * width + pair * PAIR : part * width + (pair + 1) * PAIR
                        ]

    if gathered:
        w3 = w_s[j]
        w_o[0] = w3
    else:
        w3 = jnp.concatenate([wq[...], wk[...], wv[...]], axis=1)
    qkv = mm(x_ref[...], w3)
    query = ((qkv[:rows, :PAIR] + bq[...].astype(F32)) * HEAD_DIM**-0.5).astype(BF16)
    keys = qkv[:, PAIR : 2 * PAIR].astype(BF16)
    values = (qkv[:, 2 * PAIR :] + bv[...].astype(F32)).astype(BF16)
    q_o[...] = query
    k_o[...] = keys
    v_o[...] = values
    values_t = values.astype(F32).T.astype(BF16)
    lane = lax.broadcasted_iota(jnp.int32, (1, PAIR), 1) // HEAD_DIM
    for first, count, key_first, mask, p_o in (
        (0, SEG, 0, mask_a, pa_o),
        (SEG, half, SEG, mask_m, pm_o),
    ):
        parts = []
        for h in range(2):
            query_h = jnp.where(lane == h, query[first : first + count], jnp.zeros((), BF16))
            scores = mm_nt(keys[key_first : key_first + SEG], query_h) + mask[...]
            top = jnp.max(scores, axis=0, keepdims=True)
            grown = jnp.exp(scores - top)
            probs = (grown * (1.0 / jnp.sum(grown, axis=0, keepdims=True))).astype(BF16)
            p_o[h] = probs
            parts.append(
                mm(
                    values_t[h * HEAD_DIM : (h + 1) * HEAD_DIM, key_first : key_first + SEG],
                    probs,
                )
            )
        ctx_o[first : first + count] = jnp.concatenate(parts, axis=0).T.astype(BF16)


def attend_forward(pos, x, weights, bq, bv, segs, rows, gathered):
    total = x.shape[0]
    dim = x.shape[1]
    width = bq.shape[1]
    pairs = width // PAIR
    half = rows - SEG
    column = lambda n: pl.BlockSpec((n, PAIR), lambda j, pos: (0, j))
    out_shape = [
        shape((rows, width), BF16),
        shape((total, width), BF16),
        shape((total, width), BF16),
        shape((rows, width), BF16),
        shape((2 * pairs, SEG, SEG), BF16),
        shape((2 * pairs, SEG, half), BF16),
    ]
    out_specs = [
        column(rows),
        column(total),
        column(total),
        column(rows),
        pl.BlockSpec((2, SEG, SEG), lambda j, pos: (j, 0, 0)),
        pl.BlockSpec((2, SEG, half), lambda j, pos: (j, 0, 0)),
    ]
    scratch = [pltpu.VMEM((SEG, SEG), F32), pltpu.VMEM((SEG, half), F32)]
    if gathered:
        w_specs = [whole(w) for w in weights]
        out_shape.append(shape((pairs, dim, 3 * PAIR), BF16))
        out_specs.append(pl.BlockSpec((1, dim, 3 * PAIR), lambda j, pos: (j, 0, 0)))
        scratch.append(pltpu.VMEM((pairs, dim, 3 * PAIR), BF16))
    else:
        w_specs = [column(dim) for w in weights]
    inputs = [x, *weights, bq, bv, *segs]
    specs = [whole(x), *w_specs, column(1), column(1), *[whole(s) for s in segs]]
    flops = 2 * total * dim * 3 * width + 8 * 2 * SEG * rows * width
    return call(
        functools.partial(attend_forward_body, gathered),
        (pairs,),
        pos,
        inputs,
        specs,
        out_shape,
        out_specs,
        scratch,
        flops,
        "attend_fwd_other" if gathered else "attend_fwd_own",
    )


def up_body(
    pos_ref, x, ctx_i, ctx_o, wo_i, o0, o1, oc, b_out, gain, bias, wu, bu, wd,
    normed_o, inv_o, hidden_o, wo_all, active_o, slope_o, branch_o,
):
    j = pl.program_id(0)
    rows = x.shape[0]

    @pl.when(j == 0)
    def _():
        quarter = o0.shape[0]
        for rel, piece in enumerate((o0, o1, oc.at[0], oc.at[1])):
            row = pl.multiple_of((pos_ref[0] ^ rel) * quarter, 16)
            wo_all[pl.ds(row, quarter), :] = piece[...]
        for r in range(0, rows, TILE):
            at = slice(r, r + TILE)
            first = (
                x[at].astype(F32)
                + (mm(ctx_i[at], wo_i[...]) + mm(ctx_o[at], wo_all[...]))
                + b_out[...].astype(F32)
            )
            centre = first - jnp.mean(first, axis=-1, keepdims=True)
            inverse = lax.rsqrt(jnp.mean(centre * centre, axis=-1, keepdims=True) + EPS)
            normed = centre * inverse
            normed_o[at] = normed
            inv_o[at] = inverse
            hidden_o[at] = (normed * gain[...].astype(F32) + bias[...].astype(F32)).astype(BF16)

    for r in range(0, rows, TILE):
        at = slice(r, r + TILE)
        inner = mm(hidden_o[at], wu[...]) + bu[...].astype(F32)
        active, slope = gelu_parts(inner)
        active = active.astype(BF16)
        active_o[at] = active
        slope_o[at] = slope.astype(BF16)
        add = mm(active, wd[...])

        @pl.when(j == 0)
        def _():
            branch_o[at] = add

        @pl.when(j > 0)
        def _():
            branch_o[at] += add


def down_body(
    pos_ref, hidden, branch, u0, u1, uc, d0, d1, dc, bu, b_down, gain, bias, cot, keep,
    active_o, slope_o, out_o, grad_o, low_o, vec_o, wu, wd, acc,
):
    j = pl.program_id(0)
    rows = hidden.shape[0]

    @pl.when(j == 0)
    def _():
        wu[...] = u0[...]
        wd[...] = d0[...]
        acc[...] = branch[...]

    @pl.when(j == 1)
    def _():
        wu[...] = u1[...]
        wd[...] = d1[...]

    @pl.when(j > 1)
    def _():
        wu[...] = uc[0]
        wd[...] = dc[0]

    for r in range(0, rows, TILE):
        at = slice(r, r + TILE)
        inner = mm(hidden[at], wu[...]) + bu[...].astype(F32)
        active, slope = gelu_parts(inner)
        active = active.astype(BF16)
        active_o[at] = active
        slope_o[at] = slope.astype(BF16)
        acc[at] += mm(active, wd[...])

    @pl.when(j == pl.num_programs(0) - 1)
    def _():
        sums = [0.0, 0.0, 0.0]
        for r in range(0, rows, TILE):
            at = slice(r, r + TILE)
            second = hidden[at].astype(F32) + acc[at] + b_down[...].astype(F32)
            centre = second - jnp.mean(second, axis=-1, keepdims=True)
            inverse = lax.rsqrt(jnp.mean(centre * centre, axis=-1, keepdims=True) + EPS)
            normed = centre * inverse
            g = gain[...].astype(F32)
            out_o[at] = ((normed * g + bias[...].astype(F32)) * keep[at]).astype(BF16)
            upstream = cot[at].astype(F32) * keep[at]
            scaled = upstream * g
            grad = inverse * (
                scaled
                - jnp.mean(scaled, axis=-1, keepdims=True)
                - normed * jnp.mean(scaled * normed, axis=-1, keepdims=True)
            )
            grad_o[at] = grad
            low_o[at] = grad.astype(BF16)
            sums[0] += jnp.sum(upstream * normed, axis=0, keepdims=True)
            sums[1] += jnp.sum(upstream, axis=0, keepdims=True)
            sums[2] += jnp.sum(grad, axis=0, keepdims=True)
        for i, value in enumerate(sums):
            vec_o[i : i + 1] = value


def ffn_back_body(gathered, pos_ref, low, hidden, active, slope, *refs):
    if gathered:
        u0, u1, uc, d0, d1, dc, hg_in = refs[:7]
        hg, send, keep, bup, low_t, hidden_t, ig, grads, wu, wd = refs[7:]
    else:
        wu, wd, hg_in = refs[:3]
        hg, send, keep, bup, low_t, hidden_t, ig, grads = refs[3:]
    j = pl.program_id(0)
    rows = low.shape[0]
    dim = low.shape[1]

    @pl.when(j == 0)
    def _():
        low_t[...] = low[...].T
        hidden_t[...] = hidden[...].T
        hg[...] = hg_in[...]

    if gathered:

        @pl.when(j < 2)
        def _():
            wu[...] = uc[0]
            wd[...] = dc[0]

        @pl.when(j == 2)
        def _():
            wu[...] = u0[...]
            wd[...] = d0[...]

        @pl.when(j == 3)
        def _():
            wu[...] = u1[...]
            wd[...] = d1[...]

    total = 0.0
    for r in range(0, rows, TILE):
        at = slice(r, r + TILE)
        inner_grad = (mm_nt(low[at], wd[...]) * slope[at].astype(F32)).astype(BF16)
        ig[at] = inner_grad
        total += jnp.sum(inner_grad.astype(F32), axis=0, keepdims=True)
        hg[at] += mm_nt(inner_grad, wu[...])
    bup[0] = total
    for r in range(0, dim, TILE):
        grads[r : r + TILE] = mm(hidden_t[r : r + TILE], ig[...]).astype(BF16)
        grads[dim + r : dim + r + TILE] = mm(low_t[r : r + TILE], active[...]).astype(BF16)

    @pl.when(j < 2)
    def _():
        send[0] = grads[...]

    @pl.when(j >= 2)
    def _():
        keep[0] = grads[...]


def ffn_back(pos, low, hidden, active, slope, weights, hg_in, gathered):
    rows, dim = low.shape
    width = active.shape[1]
    quarter = width // 4
    chunk = lambda n: pl.BlockSpec((n, quarter), lambda j, pos: (0, j ^ 2))
    scratch = [
        pltpu.VMEM((dim, rows), BF16),
        pltpu.VMEM((dim, rows), BF16),
        pltpu.VMEM((rows, quarter), BF16),
        pltpu.VMEM((2 * dim, quarter), BF16),
    ]
    if gathered:
        u0, u1, uc, d0, d1, dc = weights
        w_specs = [
            whole(u0),
            whole(u1),
            pl.BlockSpec((1, dim, quarter), lambda j, pos: (jnp.minimum(j, 1), 0, 0)),
            whole(d0),
            whole(d1),
            pl.BlockSpec((1, quarter, dim), lambda j, pos: (jnp.minimum(j, 1), 0, 0)),
        ]
        scratch += [pltpu.VMEM((dim, quarter), BF16), pltpu.VMEM((quarter, dim), BF16)]
    else:
        w_specs = [
            pl.BlockSpec((dim, quarter), lambda j, pos: (0, pos[0] ^ j ^ 2)),
            pl.BlockSpec((quarter, dim), lambda j, pos: (pos[0] ^ j ^ 2, 0)),
        ]
    piece = (2, 2 * dim, quarter)
    return call(
        functools.partial(ffn_back_body, gathered),
        (4,),
        pos,
        [low, hidden, active, slope, *weights, hg_in],
        [whole(low), whole(hidden), chunk(rows), chunk(rows), *w_specs, whole(hg_in)],
        [
            shape((rows, dim), F32),
            shape(piece, BF16),
            shape(piece, BF16),
            shape((4, 1, quarter), F32),
        ],
        [
            pl.BlockSpec((rows, dim), lambda j, pos: (0, 0)),
            pl.BlockSpec((1, 2 * dim, quarter), lambda j, pos: (jnp.minimum(j, 1), 0, 0)),
            pl.BlockSpec((1, 2 * dim, quarter), lambda j, pos: (jnp.maximum(j - 2, 0), 0, 0)),
            pl.BlockSpec((1, 1, quarter), lambda j, pos: (pos[0] ^ j ^ 2, 0, 0)),
        ],
        scratch,
        8 * rows * dim * width,
        "ffn_back_other" if gathered else "ffn_back_own",
    )


def out_back_body(
    pos_ref, hg, normed, inv, gain, wo_i, wo_o, ctx_i, ctx_o,
    first_o, dctx_i, dctx_o, keep_i, send_i, keep_o, send_o, vec_o, low_s, low_t,
):
    rows, dim = hg.shape
    sums = [0.0, 0.0, 0.0]
    for r in range(0, rows, TILE):
        at = slice(r, r + TILE)
        grad_in = hg[at]
        n = normed[at]
        scaled = grad_in * gain[...].astype(F32)
        grad = inv[at] * (
            scaled
            - jnp.mean(scaled, axis=-1, keepdims=True)
            - n * jnp.mean(scaled * n, axis=-1, keepdims=True)
        )
        first_o[at] = grad
        low = grad.astype(BF16)
        low_s[at] = low
        dctx_i[at] = mm_nt(low, wo_i[...]).astype(BF16)
        dctx_o[at] = mm_nt(low, wo_o[...]).astype(BF16)
        sums[0] += jnp.sum(grad_in * n, axis=0, keepdims=True)
        sums[1] += jnp.sum(grad_in, axis=0, keepdims=True)
        sums[2] += jnp.sum(grad, axis=0, keepdims=True)
    for i, value in enumerate(sums):
        vec_o[i : i + 1] = value
    low_t[...] = low_s[...].T
    quarter = dim // 4
    for rel in range(4):
        row = pl.multiple_of((pos_ref[0] ^ rel) * quarter, 16)
        block = low_t[pl.ds(row, quarter), :]
        at = slice((rel % 2) * quarter, (rel % 2 + 1) * quarter)
        (keep_i if rel < 2 else send_i)[at] = mm(block, ctx_i[...]).astype(BF16)
        (keep_o if rel < 2 else send_o)[at] = mm(block, ctx_o[...]).astype(BF16)


def attend_back_body(
    gathered, last, pos_ref, x, q, k, v, p_a, p_m, dctx, ctx, *refs
):
    if gathered:
        w3, refs = refs[0], refs[1:]
    else:
        (wq, wk, wv), refs = refs[:3], refs[3:]
    if last:
        (tot_in, first), refs = refs[:2], refs[2:]
    gk, gs, tot, keep, send, bq, bv, x_tmp, x_t, d3 = refs
    j = pl.program_id(0)
    rows = q.shape[0]
    total, dim = x.shape
    half = rows - SEG
    quarter = dim // 4

    @pl.when(j == 0)
    def _():
        x_tmp[...] = x[...].T
        for rel in range(4):
            row = pl.multiple_of((pos_ref[0] ^ rel) * quarter, 16)
            x_t[rel * quarter : (rel + 1) * quarter] = x_tmp[pl.ds(row, quarter), :]
        if last:
            tot[...] = tot_in[...]
            tot[:rows] += first[...]
        else:
            tot[...] = jnp.zeros_like(tot)
        d3[rows:, :PAIR] = jnp.zeros((total - rows, PAIR), BF16)

    @pl.when(j < 3)
    def _():
        lane = lax.broadcasted_iota(jnp.int32, (1, PAIR), 1) // HEAD_DIM
        zero = jnp.zeros((), BF16)
        delta_t = (dctx[...].astype(F32) * ctx[...].astype(F32)).T
        keys_t = k[...].astype(F32).T.astype(BF16)
        for first_row, count, key_first, p in ((0, SEG, 0, p_a), (SEG, half, SEG, p_m)):
            at = slice(first_row, first_row + count)
            ks = slice(key_first, key_first + SEG)
            values_grad = keys_grad = 0.0
            query_parts = []
            for h in range(2):
                grad_h = jnp.where(lane == h, dctx[at], zero)
                query_h = jnp.where(lane == h, q[at], zero)
                probs = p[h]
                delta = jnp.sum(
                    delta_t[h * HEAD_DIM : (h + 1) * HEAD_DIM, at], axis=0, keepdims=True
                )
                prob_grad = mm_nt(v[ks], grad_h)
                score_grad = (probs.astype(F32) * (prob_grad - delta)).astype(BF16)
                values_grad += mm(probs, grad_h)
                keys_grad += mm(score_grad, query_h)
                query_parts.append(
                    mm(keys_t[h * HEAD_DIM : (h + 1) * HEAD_DIM, ks], score_grad)
                )
            query_grad = jnp.concatenate(query_parts, axis=0).T * HEAD_DIM**-0.5
            d3[at, :PAIR] = query_grad.astype(BF16)
            d3[ks, PAIR : 2 * PAIR] = keys_grad.astype(BF16)
            d3[ks, 2 * PAIR :] = values_grad.astype(BF16)
        bq[...] = jnp.sum(d3[:rows, :PAIR].astype(F32), axis=0, keepdims=True)
        bv[...] = jnp.sum(d3[:, 2 * PAIR :].astype(F32), axis=0, keepdims=True)
        if gathered:
            w = w3[0]
        else:
            w = jnp.concatenate([wq[...], wk[...], wv[...]], axis=1)
        tot[...] += mm_nt(d3[...], w)
        keep[...] = mm(x_t[: 2 * quarter], d3[...]).astype(BF16)
        send[...] = mm(x_t[2 * quarter :], d3[...]).astype(BF16)

    @pl.when(j == 3)
    def _():
        keep[...] = gk[...]
        send[...] = gs[...]


def attend_back(pos, x, saved, dctx, weights, sums, grads, gathered, last):
    q, k, v, ctx, p_a, p_m = saved
    rows, width = q.shape
    total, dim = x.shape
    half = rows - SEG
    pairs = width // PAIR
    column = lambda n: pl.BlockSpec((n, PAIR), lambda j, pos: (0, jnp.minimum(j, pairs - 1)))
    plane = lambda a, b, c: pl.BlockSpec(
        (a, b, c), lambda j, pos: (jnp.minimum(j, pairs - 1), 0, 0)
    )
    if gathered:
        w_specs = [plane(1, dim, 3 * PAIR)]
    else:
        w_specs = [column(dim)] * 3
    out = pl.BlockSpec((dim // 2, 3 * PAIR), lambda j, pos: (0, j))
    return call(
        functools.partial(attend_back_body, gathered, last),
        (pairs + 1,),
        pos,
        [x, q, k, v, p_a, p_m, dctx, ctx, *weights, *sums, *grads],
        [
            whole(x),
            column(rows),
            column(total),
            column(total),
            plane(2, SEG, SEG),
            plane(2, SEG, half),
            column(rows),
            column(rows),
            *w_specs,
            *[whole(s) for s in sums],
            *[whole(g) for g in grads],
        ],
        [
            shape((total, dim), F32),
            shape((dim // 2, 3 * width + 3 * PAIR), BF16),
            shape((dim // 2, 3 * width + 3 * PAIR), BF16),
            shape((1, width), F32),
            shape((1, width), F32),
        ],
        [
            pl.BlockSpec((total, dim), lambda j, pos: (0, 0)),
            out,
            out,
            column(1),
            column(1),
        ],
        [
            pltpu.VMEM((dim, total), BF16),
            pltpu.VMEM((dim, total), BF16),
            pltpu.VMEM((total, 3 * PAIR), BF16),
        ],
        2 * total * dim * 3 * width * 2 + 16 * 2 * SEG * rows * width,
        "attend_back_other" if gathered else "attend_back_own",
    )


def ffn_final_body(pos_ref, a, b, c, up_o, down_o):
    j = pl.program_id(0)
    dim = up_o.shape[0]

    def put(piece):
        up_o[...] = piece[:dim].astype(F32)
        down_o[...] = piece[dim:].astype(F32).T

    @pl.when(j == 0)
    def _():
        put(a)

    @pl.when(j == 1)
    def _():
        put(b)

    @pl.when(j > 1)
    def _():
        put(c.at[0])


def att_final_body(pos_ref, a, b, c, q_o, k_o, v_o, out_o, tmp):
    quarter = a.shape[0]
    width = q_o.shape[1]
    for rel, piece in enumerate((a, b, c.at[0], c.at[1])):
        row = pl.multiple_of((pos_ref[0] ^ rel) * quarter, 16)
        for part, ref in enumerate((q_o, k_o, v_o)):
            for pair in range(width // PAIR):
                ref[pl.ds(row, quarter), pair * PAIR : (pair + 1) * PAIR] = piece[
                    :, (3 * pair + part) * PAIR : (3 * pair + part + 1) * PAIR
                ].astype(F32)
        tmp[pl.ds(row, quarter), :] = piece[:, 3 * width :].astype(F32)
    out_o[...] = tmp[...].T


def row_layout(bucket, lens, places):
    span = jnp.where(bucket == 0, SEG, jnp.where(bucket == 1, SEG // 2, SEG // 4)).astype(jnp.int32)
    row_ids = places // span
    slots = jnp.arange(4, dtype=jnp.int32)
    row_len = jnp.sum(jnp.where(row_ids[:, None] == slots[None, :], lens[None, :], 0), axis=1)
    return row_ids, places - row_ids * span < row_len


def swap(value, axis):
    return lax.ppermute(value, axis, [(0, 1), (1, 0)])


def shards(
    depth,
    tokens, lengths, buckets, w_query, b_query, w_key, w_value, b_value, w_out, b_out,
    norm1_gain, norm1_bias, w_up, b_up, w_down, b_down, norm2_gain, norm2_bias, cotangent,
):
    iz, ix, ic, iy = (lax.axis_index(a) for a in ("z", "x", "c", "y"))
    place = 2 * ic + ix
    pos = place.astype(jnp.int32).reshape(1)
    rows, dim = tokens.shape
    half = rows - SEG
    width = w_query.shape[1]
    units = w_up.shape[1]
    chunk = units // 4
    same = ic == iy

    def own_rows(value):
        full = lax.dynamic_slice_in_dim(value, iy * half, SEG)
        middle = lax.dynamic_slice_in_dim(value, (1 - iy) * SEG, half)
        return full, middle

    x_full, x_mid = own_rows(tokens)
    from_y = lax.ppermute(x_mid, ("c", "y"), [(1, 0), (2, 3)])
    from_c = lax.ppermute(jnp.stack([x_mid, from_y]), ("c", "y"), [(0, 2), (3, 1)])
    x = jnp.concatenate(
        [x_full, jnp.where(same, x_mid, from_c[1]), jnp.where(same, from_y, from_c[0])]
    )

    def gather(piece):
        a = swap(piece, "y")
        b = swap(a, "x")
        return a, b, swap(jnp.stack([a, b]), "c")

    def rows_at(w):
        return lax.dynamic_slice_in_dim(w, place * (w.shape[0] // 4), w.shape[0] // 4)

    bias_own = jnp.concatenate([b_query, b_value, b_up])[None]
    bias_other = swap(bias_own, "y")
    w_qkv = gather(
        jnp.concatenate([rows_at(w_query), rows_at(w_key), rows_at(w_value)], axis=1)
    )
    w_o = gather(rows_at(w_out))
    w_u = gather(lax.dynamic_slice_in_dim(w_up, place * chunk, chunk, axis=1))
    w_d = gather(rows_at(w_down))

    info = jnp.concatenate([buckets[1:2], lengths[1]]).reshape(1, 5)
    info = jnp.where(same, info, swap(info, "c"))[0]
    places = jnp.arange(SEG, dtype=jnp.int32)
    block = 2 * iy
    ids_a, ok_a = row_layout(
        lax.dynamic_index_in_dim(buckets, block, keepdims=False),
        lax.dynamic_index_in_dim(lengths, block, keepdims=False),
        places,
    )
    ids_m, ok_m = row_layout(info[0], info[1:], (places + half * ic) % SEG)
    segs = (
        ids_a[None],
        jnp.where(ok_a, ids_a, -1)[:, None],
        ids_m[None, :half],
        jnp.where(ok_m, ids_m, -1)[:, None],
    )
    keep = jnp.concatenate([ok_a, ok_m[:half]]).astype(F32)[:, None]

    cot_full, cot_mid = own_rows(cotangent)
    crossed = lambda value: lax.ppermute(value, ("c", "y"), [(1, 2), (2, 1)])
    cot = jnp.concatenate([cot_full, jnp.where(same, cot_mid, crossed(cot_mid))])

    own = attend_forward(
        pos, x, (w_query, w_key, w_value), b_query[None], b_value[None], segs, rows, False
    )
    other = attend_forward(
        pos, x, w_qkv, bias_other[:, :width], bias_other[:, width : 2 * width], segs, rows, True
    )
    w3_other = other[6]
    ctx_i, ctx_o = own[3], other[3]
    row_vec = lambda v: v[None]
    const = lambda *dims: pl.BlockSpec(dims, lambda j, pos: (0,) * len(dims))
    cols = pl.BlockSpec((rows, chunk), lambda j, pos: (0, j))
    b_out1, g1, s1 = row_vec(b_out), row_vec(norm1_gain), row_vec(norm1_bias)
    normed1, inverse1, hidden, wo_other, act_i, slope_i, branch = call(
        up_body,
        (4,),
        pos,
        [x, ctx_i, ctx_o, w_out, *w_o, b_out1, g1, s1, w_up, b_up[None], w_down],
        [
            const(rows, dim),
            whole(ctx_i),
            whole(ctx_o),
            whole(w_out),
            *[whole(w) for w in w_o],
            whole(b_out1),
            whole(g1),
            whole(s1),
            pl.BlockSpec((dim, chunk), lambda j, pos: (0, pos[0] ^ j)),
            pl.BlockSpec((1, chunk), lambda j, pos: (0, pos[0] ^ j)),
            pl.BlockSpec((chunk, dim), lambda j, pos: (pos[0] ^ j, 0)),
        ],
        [
            shape((rows, dim), F32),
            shape((rows, 1), F32),
            shape((rows, dim), BF16),
            shape((width, dim), BF16),
            shape((rows, units), BF16),
            shape((rows, units), BF16),
            shape((rows, dim), F32),
        ],
        [const(rows, dim), const(rows, 1), const(rows, dim), const(width, dim), cols, cols, const(rows, dim)],
        [],
        2 * rows * dim * (dim + 2 * units),
        "ffn_fwd_own",
    )
    pick = lambda *dims: pl.BlockSpec((1, *dims), lambda j, pos: (jnp.maximum(j - 2, 0), 0, 0))
    b_down1, g2, s2 = row_vec(b_down), row_vec(norm2_gain), row_vec(norm2_bias)
    b_up_other = bias_other[:, 2 * width :]
    act_o, slope_o, output, second, low, vec2 = call(
        down_body,
        (4,),
        pos,
        [hidden, branch, *w_u, *w_d, b_up_other, b_down1, g2, s2, cot, keep],
        [
            whole(hidden),
            whole(branch),
            whole(w_u[0]),
            whole(w_u[1]),
            pick(dim, chunk),
            whole(w_d[0]),
            whole(w_d[1]),
            pick(chunk, dim),
            pl.BlockSpec((1, chunk), lambda j, pos: (0, pos[0] ^ j)),
            whole(b_down1),
            whole(g2),
            whole(s2),
            whole(cot),
            whole(keep),
        ],
        [
            shape((rows, units), BF16),
            shape((rows, units), BF16),
            shape((rows, dim), BF16),
            shape((rows, dim), F32),
            shape((rows, dim), BF16),
            shape((3, dim), F32),
        ],
        [cols, cols, const(rows, dim), const(rows, dim), const(rows, dim), const(3, dim)],
        [pltpu.VMEM((dim, chunk), BF16), pltpu.VMEM((chunk, dim), BF16), pltpu.VMEM((rows, dim), F32)],
        4 * rows * dim * units,
        "ffn_fwd_other",
    )
    out_mid = output[SEG:]
    out_mid = jnp.where(same, out_mid, crossed(out_mid))

    def place_rows(full, middle):
        return jnp.where(
            iy == 0, jnp.concatenate([full, middle]), jnp.concatenate([middle, full])
        )

    output = place_rows(output[:SEG], out_mid)

    def start_other(send, keep_part):
        return keep_part.astype(F32) + swap(send, "c").astype(F32)

    def z_sum(value):
        step = 1
        while step < depth:
            n = value.shape[0] // 2
            bit = (iz // step) % 2
            links = [(i, i ^ step) for i in range(depth)]
            out = lax.dynamic_slice_in_dim(value, (1 - bit) * n, n)
            kept = lax.dynamic_slice_in_dim(value, bit * n, n)
            got = lax.ppermute(out, "z", links)
            value = (kept.astype(F32) + got.astype(F32)).astype(BF16)
            step *= 2
        while step > 1:
            step //= 2
            bit = (iz // step) % 2
            got = lax.ppermute(value, "z", [(i, i ^ step) for i in range(depth)])
            value = jnp.where(
                bit == 0, jnp.concatenate([value, got]), jnp.concatenate([got, value])
            )
        return value

    def reduce_parts(own_grads, other_grads, parts, size):
        send_i, keep_i = own_grads
        send_o, keep_o = other_grads
        got_o = swap(send_o, "c")
        got_i = swap(send_i, "c")
        firsts, seconds = [], []
        for n in range(parts):
            at = slice(n * size // parts, (n + 1) * size // parts)
            mine = (keep_o[:, at].astype(F32) + got_o[:, at].astype(F32)).astype(BF16)
            got_y = swap(mine, "y").astype(F32)
            kept = keep_i[:, at].astype(F32) + got_i[:, at].astype(F32) + got_y
            kept0, kept1 = kept[0].astype(BF16), kept[1].astype(BF16)
            mine = (kept0.astype(F32) + swap(kept1, "x").astype(F32)).astype(BF16)
            mine = z_sum(mine)
            firsts.append(mine)
            seconds.append(swap(mine, "x"))
        a = jnp.concatenate(firsts)
        b = jnp.concatenate(seconds)
        return a, b, swap(jnp.stack([a, b]), "c")

    hg, send_o, keep_o, bup_o = ffn_back(
        pos, low, hidden, act_o, slope_o, (*w_u, *w_d), second, True
    )
    hg, send_i, keep_i, bup_i = ffn_back(
        pos, low, hidden, act_i, slope_i, (w_up, w_down), hg, False
    )
    ffn = reduce_parts((send_i, keep_i), (send_o, keep_o), FFN_PARTS, 2 * dim)
    quarter = dim // 4
    part = (2 * quarter, width)
    first, dctx_i, dctx_o, ko_i, so_i, ko_o, so_o, vec1 = call(
        out_back_body,
        (1,),
        pos,
        [hg, normed1, inverse1, g1, w_out, wo_other, ctx_i, ctx_o],
        [whole(v) for v in (hg, normed1, inverse1, g1, w_out, wo_other, ctx_i, ctx_o)],
        [
            shape((rows, dim), F32),
            shape((rows, width), BF16),
            shape((rows, width), BF16),
            shape(part, BF16),
            shape(part, BF16),
            shape(part, BF16),
            shape(part, BF16),
            shape((3, dim), F32),
        ],
        [
            const(rows, dim),
            const(rows, width),
            const(rows, width),
            const(*part),
            const(*part),
            const(*part),
            const(*part),
            const(3, dim),
        ],
        [pltpu.VMEM((rows, dim), BF16), pltpu.VMEM((dim, rows), BF16)],
        4 * rows * dim * dim,
        "out_back",
    )
    total, ak_o, as_o, bq_o, bv_o = attend_back(
        pos, x, other[:6], dctx_o, (w3_other,), (), (ko_o, so_o), True, False
    )
    total, ak_i, as_i, bq_i, bv_i = attend_back(
        pos, x, own[:6], dctx_i, (w_query, w_key, w_value), (total, first), (ko_i, so_i), False, True
    )
    pieces = lambda v: v.reshape(2, quarter, v.shape[1])
    att = reduce_parts(
        (pieces(as_i), pieces(ak_i)), (pieces(as_o), pieces(ak_o)), ATT_PARTS, quarter
    )

    in_mid = total[SEG:rows] + swap(total[rows:].astype(BF16), "c").astype(F32)
    in_mid = jnp.where(same, in_mid, crossed(in_mid.astype(BF16)).astype(F32))
    input_grad = place_rows(total[:SEG], in_mid)

    def both(mine, theirs):
        return jnp.where(iy == 0, jnp.concatenate([mine, theirs]), jnp.concatenate([theirs, mine]))

    vec = jnp.concatenate(
        [
            both(bup_i.reshape(-1), bup_o.reshape(-1)).reshape(-1, dim),
            both(bq_i[0], bq_o[0]).reshape(-1, dim),
            both(bv_i[0], bv_o[0]).reshape(-1, dim),
            vec1,
            vec2,
        ]
    )
    for axis in ("c", "y", "x"):
        vec = vec + swap(vec, axis)
    step = 1
    while step < depth:
        vec = vec + lax.ppermute(vec, "z", [(i, i ^ step) for i in range(depth)])
        step *= 2
    up_rows = 2 * units // dim
    split = lambda v: lax.dynamic_slice_in_dim(v.reshape(-1), iy * (v.size // 2), v.size // 2)
    b_up_grad = split(vec[:up_rows])
    b_query_grad = split(vec[up_rows : up_rows + 1])
    b_value_grad = split(vec[up_rows + 1 : up_rows + 2])
    rest = vec[up_rows + 2 :]

    w_up_grad, w_down_grad = call(
        ffn_final_body,
        (4,),
        pos,
        list(ffn),
        [whole(ffn[0]), whole(ffn[1]), pick(2 * dim, chunk)],
        [shape((dim, units), F32), shape((units, dim), F32)],
        [
            pl.BlockSpec((dim, chunk), lambda j, pos: (0, pos[0] ^ j)),
            pl.BlockSpec((chunk, dim), lambda j, pos: (pos[0] ^ j, 0)),
        ],
        [],
        0,
        "ffn_final",
    )
    w_query_grad, w_key_grad, w_value_grad, w_out_grad = call(
        att_final_body,
        (1,),
        pos,
        list(att),
        [whole(v) for v in att],
        [shape((dim, width), F32)] * 3 + [shape((width, dim), F32)],
        [const(dim, width)] * 3 + [const(width, dim)],
        [pltpu.VMEM((dim, width), F32)],
        0,
        "att_final",
    )
    return (
        output,
        input_grad,
        w_query_grad,
        b_query_grad,
        w_key_grad,
        w_value_grad,
        b_value_grad,
        w_out_grad,
        rest[2],
        rest[0],
        rest[1],
        w_up_grad,
        b_up_grad,
        w_down_grad,
        rest[5],
        rest[3],
        rest[4],
    )


def solution(mesh):
    depth = mesh.shape["dp"] // 4
    inner = Mesh(mesh.devices.reshape(depth, 2, 2, mesh.shape["mp"]), ("z", "x", "c", "y"))
    dp = ("z", "x", "c")
    every = (*dp, "y")
    placed = (
        P(every, None),
        P(dp, None),
        P(dp),
        P(None, "y"),
        P("y"),
        P(None, "y"),
        P(None, "y"),
        P("y"),
        P("y", None),
        P(),
        P(),
        P(),
        P(None, "y"),
        P("y"),
        P("y", None),
        P(),
        P(),
        P(),
        P(every, None),
    )
    return jax.shard_map(
        functools.partial(shards, depth),
        mesh=inner,
        in_specs=placed,
        out_specs=(
            P(every, None),
            P(every, None),
            P(None, "y"),
            P("y"),
            P(None, "y"),
            P(None, "y"),
            P("y"),
            P("y", None),
            P(),
            P(),
            P(),
            P(None, "y"),
            P("y"),
            P("y", None),
            P(),
            P(),
            P(),
        ),
        check_vma=False,
    )
```

time: 832 us -> 509 us (0.61)
  waiting for transfers between devices: 403 us -> 143 us
  Pallas kernels: 0 us -> 154 us
  matrix products: 148 us -> 0 us
  starting transfers between devices: 0.89 us -> 111 us
  blocking collectives: 101 us -> 0 us
  local copies, waits for them, and re-layouts: 91.8 us -> 39.8 us
  between operations: 14.6 us -> 3.18 us
    psum x1 -> x0, waiting for transfers between devices: 170 us -> none  [shards(): lax.psum((w_query_grad, b_query_grad, w_key_grad, w_value_grad, b_value_g...]
    pallas_call x0 -> x11, Pallas kernels: none -> 154 us  [call(): pl.pallas_call(body, grid_spec=pltpu.PrefetchScalarGridSpec(num_scalar_pr...]
    dot_general x39 -> x0, matrix products: 148 us -> none  [the longest x1 25.4 us: forward_pass(): jnp.dot(hidden_rows, w_up, preferred_element_type=jnp.float32)]
    all_gather x4 -> x0, waiting for transfers between devices: 145 us -> none  [the longest x1 38.4 us: forward_pass(): gathered = lax.all_gather(tokens, 'mp', axis=0, tiled=True)]
    ppermute x0 -> x73, waiting for transfers between devices: none -> 143 us  [the longest x42 103 us: swap(): return lax.ppermute(value, axis, [(0, 1), (1, 0)])]
    ppermute x0 -> x73, starting transfers between devices: none -> 111 us  [the longest x42 54 us: swap(): return lax.ppermute(value, axis, [(0, 1), (1, 0)])]
    psum x2 -> x0, blocking collectives: 101 us -> none  [the longest x1 59.3 us: shards(): lax.psum((w_query_grad, b_query_grad, w_key_grad, w_value_grad, b_value_g...]
    reduce_scatter x4 -> x0, waiting for transfers between devices: 87 us -> none  [the longest x1 34.8 us: shards(): lax.psum_scatter(jnp.einsum('tf,df->td', inner_grad, w_up, preferred_elem...]
  transfers between devices with their start and end apart: 9 -> 73, of which waited for: 8 -> 36; matrix products, arithmetic and copies ran while one was open for 6% -> 17% of each run, Pallas kernels for 0% -> 13%
where the time goes in v1:
time: 509 us; the launch traced here: 502 us
  Pallas kernels  154 us (30%)
  waiting for transfers between devices  143 us (28%)
  starting transfers between devices  111 us (22%)
  other arithmetic  50.7 us (10%)
  local copies, waits for them, and re-layouts  39.8 us (8%)
    pallas_call x11, Pallas kernels, call(): pl.pallas_call(body, grid_spec=pltpu.PrefetchScalarGridSpec(num_scalar_pr...  154 us
    ppermute x42, waiting for transfers between devices, swap(): return lax.ppermute(value, axis, [(0, 1), (1, 0)])  103 us
    ppermute x42, starting transfers between devices, swap(): return lax.ppermute(value, axis, [(0, 1), (1, 0)])  54 us
    ppermute x12, starting transfers between devices, z_sum(): got = lax.ppermute(out, 'z', links)  24.8 us
    ppermute x12, waiting for transfers between devices, z_sum(): got = lax.ppermute(value, 'z', [(i, i ^ step) for i in range(depth)])  24.1 us
    ppermute x3, starting transfers between devices, shards(): crossed = lambda value: lax.ppermute(value, ('c', 'y'), [(1, 2), (2, 1)])  13.4 us
  transfers between devices with their start and end apart: 73, of which 36 were waited for; matrix products, arithmetic and copies ran while one was open for 17% of the time, Pallas kernels for 13%

profile of v1, /device:TPU:1, one launch (start us, length us, event | category | flops | bytes accessed | tf_op | source)
XLA Modules:
  0.0 501.7 jit_solution(2140961259121689323)
XLA Ops:
  6.4 4.7 collective-permute-start
  15.6 1.9 constant_dynamic-slice_fusion.17
  19.4 1.9 constant_dynamic-slice_fusion.14
  25.2 1.9 constant_dynamic-slice_fusion.16
  37.6 4.4 fusion.10.refs_8_
  43.7 4.2 fusion.13.refs_6_
  53.5 2.9 collective-permute-start.16
  59.5 2.0 collective-permute-done.3.refs_0_
  62.3 3.9 collective-permute-done.16
  72.1 2.2 pad_maximum_fusion.7
  74.3 3.9 collective-permute-start.5
  78.2 6.6 %collective-permute-done.11.u1.refs_1_ = bf16[768,384]{1,0:T(8,128)(2,1)S(1)} collective-permute-done((bf16[768,384]{1,0:T(8,128)(2,1)}, bf16[768,384]{1,0:T(8,128)(2,1)S(1)}, u32[]{:S(2)}, u32[]{:S(2)}) %collective-permute-start.11) | collective-permute-done | bytes 589856 | tf_op jit(solution)/shard_map/ppermute | solution.py:602
  86.2 3.9 collective-permute-start.12
  90.1 7.3 %collective-permute-done.14.d1.refs_4_ = bf16[384,768]{1,0:T(8,128)(2,1)S(1)} collective-permute-done((bf16[384,768]{1,0:T(8,128)(2,1)}, bf16[384,768]{1,0:T(8,128)(2,1)S(1)}, u32[]{:S(2)}, u32[]{:S(2)}) %collective-permute-start.14) | collective-permute-done | bytes 589856 | tf_op jit(solution)/shard_map/ppermute | solution.py:602
  97.4 2.4 pad_maximum_fusion.3
  99.8 2.1 collective-permute-start.15
  103.4 12.8 %attend_fwd_own.1 = (bf16[768,384]{1,0:T(8,128)(2,1)}, bf16[1024,384]{1,0:T(8,128)(2,1)}, bf16[1024,384]{1,0:T(8,128)(2,1)}, bf16[768,384]{1,0:T(8,128)(2,1)}, b...) custom-call(s32[1]{0:T(128)} %bitcast.pos_ref, bf16[1024,768]{1,0:T(8,128)(2,1)} %pad_maximum_fusion.1.x_ref.x, ...), custom_call_target="tpu_custom_call" | custom-call | flops 4227858432 | bytes 10822144 | tf_op jit(solution)/shard_map/attend_fwd_own/pallas_call | solution.py:37
  116.3 13.4 %attend_fwd_other.1 = (bf16[768,384]{1,0:T(8,128)(2,1)}, bf16[1024,384]{1,0:T(8,128)(2,1)}, bf16[1024,384]{1,0:T(8,128)(2,1)}, bf16[768,384]{1,0:T(8,128)(2,1)},...) custom-call(s32[1]{0:T(128)} %bitcast.pos_ref, ...), custom_call_target="tpu_custom_call" | custom-call | flops 4227858432 | bytes 12591616 | tf_op jit(solution)/shard_map/attend_fwd_other/pallas_call | solution.py:37
  129.7 17.6 %ffn_fwd_own.1 = (f32[768,768]{1,0:T(8,128)}, f32[768,1]{1,0:T(8,128)}, bf16[768,768]{1,0:T(8,128)(2,1)}, bf16[384,768]{1,0:T(8,128)(2,1)}, bf16[768,1536]{1,0:T...) custom-call(s32[1]{0:T(128)} %bitcast.pos_ref, bf16[1024,768]{1,0:T(8,128)(2,1)} %pad_maximum_fusion.1.x_ref.x, ...), custom_call_target="tpu_custom_call" | custom-call | flops 4529848320 | bytes 19868160 | tf_op jit(solution)/shard_map/ffn_fwd_own/pallas_call | solution.py:37
  147.3 16.4 %ffn_fwd_other.1 = (bf16[768,1536]{1,0:T(8,128)(2,1)}, bf16[768,1536]{1,0:T(8,128)(2,1)}, bf16[768,768]{1,0:T(8,128)(2,1)}, f32[768,768]{1,0:T(8,128)}, bf16[768,768]{1,0:T(8,128)(2,1)}, /*index=5*/f32[3,768]{1,0:T(4,128)}) custom-call(s32[1]{0:T(128)} %bitcast.pos_ref, bf16[768,768]{1,0:T(8,128)(2,1)} %get-tuple-element.77.hidden, ...), custom_call_target="tpu_custom_call" | custom-call | flops 3623878656 | bytes 18894336 | tf_op jit(solution)/shard_map/ffn_fwd_other/pallas_call | solution.py:37
  163.7 19.5 %ffn_back_other.1 = (f32[768,768]{1,0:T(8,128)}, bf16[2,1536,384]{2,1,0:T(8,128)(2,1)}, bf16[2,1536,384]{2,1,0:T(8,128)(2,1)}, f32[4,1,384]{2,1,0:T(1,128)}) custom-call(s32[1]{0:T(128)} %bitcast.pos_ref, bf16[768,768]{1,0:T(8,128)(2,1)} %get-tuple-element.85.low, bf16[768,768]{1,0:T(8,128)(2,1)} %get-tuple-element.77.hidden, ...), custom_call_target="tpu_custom_call" | custom-call | flops 7247757312 | bytes 21239808 | tf_op jit(solution)/shard_map/ffn_back_other/pallas_call | solution.py:37
  183.1 18.8 %ffn_back_own.1 = (f32[768,768]{1,0:T(8,128)}, bf16[2,1536,384]{2,1,0:T(8,128)(2,1)}, bf16[2,1536,384]{2,1,0:T(8,128)(2,1)}, f32[4,1,384]{2,1,0:T(1,128)}) custom-call(s32[1]{0:T(128)} %bitcast.pos_ref, bf16[768,768]{1,0:T(8,128)(2,1)} %get-tuple-element.85.low, bf16[768,768]{1,0:T(8,128)(2,1)} %get-tuple-element.77.hidden, ...), custom_call_target="tpu_custom_call" | custom-call | flops 7247757312 | bytes 21239808 | tf_op jit(solution)/shard_map/ffn_back_own/pallas_call | solution.py:37
  202.0 7.4 %out_back.1 = (f32[768,768]{1,0:T(8,128)}, bf16[768,384]{1,0:T(8,128)(2,1)}, bf16[768,384]{1,0:T(8,128)(2,1)}, bf16[384,384]{1,0:T(8,128)(2,1)}, bf16[384,384]{1...) custom-call(s32[1]{0:T(128)} %bitcast.pos_ref, ...), custom_call_target="tpu_custom_call" | custom-call | flops 1811939328 | bytes 11810304 | tf_op jit(solution)/shard_map/out_back/pallas_call | solution.py:37
  209.4 17.2 %attend_back_other.1 = (f32[1024,768]{1,0:T(8,128)}, bf16[384,1536]{1,0:T(8,128)(2,1)}, bf16[384,1536]{1,0:T(8,128)(2,1)}, f32[1,384]{1,0:T(1,128)}, f32[1,384]{1,0:T(1,128)}) custom-call(s32[1]{0:T(128)} %bitcast.pos_ref, bf16[1024,768]{1,0:T(8,128)(2,1)} %pad_maximum_fusion.1.x_ref.x, bf16[768,384]{1,0:T(8,128)(2,1)} %get-tuple-element.97.q, ...), custom_call_target="tpu_custom_call" | custom-call | flops 8455716864 | bytes 17501184 | tf_op jit(solution)/shard_map/attend_back_other/pallas_call | solution.py:37
  226.7 19.2 %attend_back_own.1 = (f32[1024,768]{1,0:T(8,128)}, bf16[384,1536]{1,0:T(8,128)(2,1)}, bf16[384,1536]{1,0:T(8,128)(2,1)}, f32[1,384]{1,0:T(1,128)}, f32[1,384]{1,0:T(1,128)}) custom-call(s32[1]{0:T(128)} %bitcast.pos_ref, bf16[1024,768]{1,0:T(8,128)(2,1)} %pad_maximum_fusion.1.x_ref.x, bf16[768,384]{1,0:T(8,128)(2,1)} %get-tuple-element.80.q, ...), custom_call_target="tpu_custom_call" | custom-call | flops 8455716864 | bytes 23006208 | tf_op jit(solution)/shard_map/attend_back_own/pallas_call | solution.py:37
  254.7 21.9 %collective-permute-done.38 = f32[12,768]{1,0:T(8,128)S(1)} collective-permute-done((f32[12,768]{1,0:T(8,128)S(1)}, f32[12,768]{1,0:T(8,128)S(1)}, u32[]{:S(2)}, u32[]{:S(2)}) %collective-permute-start.38) | collective-permute-done | bytes 36896 | tf_op jit(solution)/shard_map/ppermute | solution.py:602
  277.3 2.3 collective-permute-done.39
  280.9 2.3 collective-permute-start.43
  283.2 2.5 collective-permute-start.42
  285.7 2.4 collective-permute-start.41
  291.5 6.8 %collective-permute-done.23 = bf16[96,1536]{1,0:T(8,128)(2,1)S(1)} collective-permute-done((bf16[96,1536]{1,0:T(8,128)(2,1)S(1)}, bf16[96,1536]{1,0:T(8,128)(2,1)S(1)}, u32[]{:S(2)}, u32[]{:S(2)}) %collective-permute-start.23) | collective-permute-done | bytes 294944 | tf_op jit(solution)/shard_map/ppermute | solution.py:602
  299.7 4.8 collective-permute-done.29
  306.2 2.5 collective-permute-done.30
  309.1 2.0 collective-permute-done.25
  312.5 1.9 collective-permute-done.31
  314.6 2.0 collective-permute-done.26
  323.8 1.9 slice.378
  328.8 6.0 %collective-permute-start.18 = (bf16[256,768]{1,0:T(8,128)(2,1)}, bf16[256,768]{1,0:T(8,128)(2,1)}, u32[]{:S(2)}, u32[]{:S(2)}) collective-permute-start(bf16[256,768]{1,0:T(8,128)(2,1)} %slice.378), channel_id=1, source_target_pairs={{0,2},{2,0},{1,3},{3,1},{4,6},{6,4},{5,7},{7,5},{8,10},{10,8},{9,1... | collective-permute-start | bytes 1179656 | tf_op jit(solution)/shard_map/ppermute | solution.py:602
  334.8 8.6 %collective-permute-start.17 = (bf16[256,768]{1,0:T(8,128)(2,1)}, bf16[256,768]{1,0:T(8,128)(2,1)}, u32[]{:S(2)}, u32[]{:S(2)}) collective-permute-start(bf16[256,768]{1,0:T(8,128)(2,1)} %slice.217), channel_id=1, source_target_pairs={{1,2},{2,1},{5,6},{6,5},{9,10},{10,9},{13,14},{14,13},{17,18},{18,... | collective-permute-start | bytes 1179656 | tf_op jit(solution)/shard_map/ppermute | solution.py:668
  343.4 9.2 %collective-permute-done.56 = bf16[2,384,384]{2,1,0:T(8,128)(2,1)} collective-permute-done((bf16[2,384,384]{2,1,0:T(8,128)(2,1)}, bf16[2,384,384]{2,1,0:T(8,128)(2,1)}, u32[]{:S(2)}, u32[]{:S(2)}) %collective-permute-start.56) | collective-permute-done | bytes 589856 | tf_op jit(solution)/shard_map/ppermute | solution.py:602
  352.6 12.6 %collective-permute-done.62 = bf16[2,384,384]{2,1,0:T(8,128)(2,1)} collective-permute-done((bf16[2,384,384]{2,1,0:T(8,128)(2,1)}, bf16[2,384,384]{2,1,0:T(8,128)(2,1)}, u32[]{:S(2)}, u32[]{:S(2)}) %collective-permute-start.62) | collective-permute-done | bytes 589856 | tf_op jit(solution)/shard_map/ppermute | solution.py:602
  365.3 3.3 add_convert_fusion.6
  371.7 2.6 collective-permute-done.45
  377.4 1.9 collective-permute-start.46
  380.6 2.4 collective-permute-start.52
  383.0 3.7 collective-permute-done.63
  386.8 2.5 collective-permute-start.58
  389.5 8.8 %collective-permute-start.47 = (bf16[96,384]{1,0:T(8,128)(2,1)S(1)}, bf16[96,384]{1,0:T(8,128)(2,1)S(1)}, u32[]{:S(2)}, u32[]{:S(2)}) collective-permute-start(bf16[96,384]{1,0:T(8,128)(2,1)S(1)} %constant_dynamic-slice_fusion.6), channel_id=1, source_target_pairs={{0,16},{8,24},{16,0},{24,8},{1,17},{9,25},{17,1},{25,9},{2,18},{10... | collective-permute-start | bytes 221192 | tf_op jit(solution)/shard_map/ppermute | solution.py:773
  398.5 2.7 collective-permute-start.53
  401.2 3.2 collective-permute-start.59
  404.7 2.4 collective-permute-start.48
  410.4 6.1 %collective-permute-done.48 = bf16[96,384]{1,0:T(8,128)(2,1)S(1)} collective-permute-done((bf16[96,384]{1,0:T(8,128)(2,1)S(1)}, bf16[96,384]{1,0:T(8,128)(2,1)S(1)}, u32[]{:S(2)}, u32[]{:S(2)}) %collective-permute-start.48) | collective-permute-done | bytes 73760 | tf_op jit(solution)/shard_map/ppermute | solution.py:779
  416.5 2.3 collective-permute-done.54
  421.7 1.9 collective-permute-done.66
  427.4 2.8 collective-permute-done.61
  430.7 2.8 collective-permute-done.67
  436.5 3.6 collective-permute-done.70
  440.2 6.3 %collective-permute-done.71 = bf16[384,384]{1,0:T(8,128)(2,1)S(1)} collective-permute-done((bf16[384,384]{1,0:T(8,128)(2,1)S(1)}, bf16[384,384]{1,0:T(8,128)(2,1)S(1)}, u32[]{:S(2)}, u32[]{:S(2)}) %collective-permute-start.71) | collective-permute-done | bytes 294944 | tf_op jit(solution)/shard_map/ppermute | solution.py:602
  448.3 12.3 %collective-permute-start.72 = (bf16[2,1536,384]{2,1,0:T(8,128)(2,1)}, bf16[2,1536,384]{2,1,0:T(8,128)(2,1)}, u32[]{:S(2)}, u32[]{:S(2)}) collective-permute-start(bf16[2,1536,384]{2,1,0:T(8,128)(2,1)} %pad_maximum_fusion), channel_id=1, source_target_pairs={{0,2},{2,0},{1,3},{3,1},{4,6},{6,4},{5,7},{7,5},{8,10},{10,8},{9,1... | collective-permute-start | bytes 7077896 | tf_op jit(solution)/shard_map/ppermute | solution.py:602
  461.9 7.5 %collective-permute-done.35 = bf16[96,1536]{1,0:T(8,128)(2,1)S(1)} collective-permute-done((bf16[96,1536]{1,0:T(8,128)(2,1)S(1)}, bf16[96,1536]{1,0:T(8,128)(2,1)S(1)}, u32[]{:S(2)}, u32[]{:S(2)}) %collective-permute-start.35) | collective-permute-done | bytes 294944 | tf_op jit(solution)/shard_map/ppermute | solution.py:602
  477.8 1.9 collective-permute-start.19
  482.2 4.6 collective-permute-done.19
  489.9 4.3 att_final.1
  494.1 7.4 %ffn_final.1 = (f32[768,1536]{1,0:T(8,128)}, f32[1536,768]{1,0:T(8,128)}) custom-call(s32[1]{0:T(128)} %bitcast.pos_ref, bf16[1536,384]{1,0:T(8,128)(2,1)} %get-tuple-element.152.a, bf16[1536,384]{1,0:T(8,128)(2,1)} %copy-done, bf16[2,1536,384]{2,1,0:T(8,128)(2,1)} %collective-permute-done.72.c), custom_call_target="tpu_custom_call" | custom-call | bytes 14155776 | tf_op jit(solution)/shard_map/ffn_final/pallas_call | solution.py:37
  (300 shorter events, 112.9 us)
Async XLA Ops:
  4.6 29.0 %collective-permute-start.2 = (s32[1,5]{1,0:T(1,128)}, s32[1,5]{1,0:T(1,128)}, u32[]{:S(2)}, u32[]{:S(2)}) collective-permute-start(s32[1,5]{1,0:T(1,128)} %add_bitcast_fusion), channel_id=1, source_target_pairs={{0,2},{2,0},{1,3},{3,1},{4,6},{6,4},{5,7},{7,5},{8,10},{10,8},{9,1... | collective-permute-start | bytes 68 | tf_op jit(solution)/shard_map/ppermute | solution.py:602
  6.4 53.0 %collective-permute-start = (bf16[256,768]{1,0:T(8,128)(2,1)}, bf16[256,768]{1,0:T(8,128)(2,1)S(1)}, u32[]{:S(2)}, u32[]{:S(2)}) collective-permute-start(bf16[256,768]{1,0:T(8,128)(2,1)} %constant_dynamic-slice_fusion.23), channel_id=1, source_target_pairs={{1,0},{2,3},{5,4},{6,7},{9,8},{10,11},{13,12},{14,15},{17,16},{18,... | collective-permute-start | bytes 1179656 | tf_op jit(solution)/shard_map/ppermute | solution.py:626
  12.5 37.0 %collective-permute-start.6 = (bf16[1,2304]{1,0:T(2,128)(2,1)}, bf16[1,2304]{1,0:T(2,128)(2,1)}, u32[]{:S(2)}, u32[]{:S(2)}) collective-permute-start(bf16[1,2304]{1,0:T(2,128)(2,1)} %broadcast_in_dim.76), channel_id=1, source_target_pairs={{0,1},{1,0},{2,3},{3,2},{4,5},{5,4},{6,7},{7,6},{8,9},{9,8},{10,11... | collective-permute-start | bytes 13832 | tf_op jit(solution)/shard_map/ppermute | solution.py:602
  14.1 33.9 %collective-permute-start.7 = (bf16[96,768]{1,0:T(8,128)(2,1)}, bf16[96,768]{1,0:T(8,128)(2,1)}, u32[]{:S(2)}, u32[]{:S(2)}) collective-permute-start(bf16[96,768]{1,0:T(8,128)(2,1)} %constant_dynamic-slice_fusion.18), channel_id=1, source_target_pairs={{0,1},{1,0},{2,3},{3,2},{4,5},{5,4},{6,7},{7,6},{8,9},{9,8},{10,11... | collective-permute-start | bytes 442376 | tf_op jit(solution)/shard_map/ppermute | solution.py:602
  17.5 50.4 %collective-permute-start.10 = (bf16[768,384]{1,0:T(8,128)(2,1)}, bf16[768,384]{1,0:T(8,128)(2,1)}, u32[]{:S(2)}, u32[]{:S(2)}) collective-permute-start(bf16[768,384]{1,0:T(8,128)(2,1)} %constant_dynamic-slice_fusion.17), channel_id=1, source_target_pairs={{0,1},{1,0},{2,3},{3,2},{4,5},{5,4},{6,7},{7,6},{8,9},{9,8},{10,11... | collective-permute-start | bytes 1769480 | tf_op jit(solution)/shard_map/ppermute | solution.py:602
  33.6 34.6 %collective-permute-start.13 = (bf16[384,768]{1,0:T(8,128)(2,1)}, bf16[384,768]{1,0:T(8,128)(2,1)}, u32[]{:S(2)}, u32[]{:S(2)}) collective-permute-start(bf16[384,768]{1,0:T(8,128)(2,1)} %constant_dynamic-slice_fusion.16), channel_id=1, source_target_pairs={{0,1},{1,0},{2,3},{3,2},{4,5},{5,4},{6,7},{7,6},{8,9},{9,8},{10,11... | collective-permute-start | bytes 1769480 | tf_op jit(solution)/shard_map/ppermute | solution.py:602
  49.5 12.0 %collective-permute-start.3 = (bf16[192,1152]{1,0:T(8,128)(2,1)}, bf16[192,1152]{1,0:T(8,128)(2,1)}, u32[]{:S(2)}, u32[]{:S(2)}) collective-permute-start(bf16[192,1152]{1,0:T(8,128)(2,1)} %pad_maximum_fusion.10), channel_id=1, source_target_pairs={{0,1},{1,0},{2,3},{3,2},{4,5},{5,4},{6,7},{7,6},{8,9},{9,8},{10,11... | collective-permute-start | bytes 1327112 | tf_op jit(solution)/shard_map/ppermute | solution.py:602
  53.5 12.6 %collective-permute-start.16 = (bf16[256,768]{1,0:T(8,128)(2,1)}, bf16[256,768]{1,0:T(8,128)(2,1)S(1)}, u32[]{:S(2)}, u32[]{:S(2)}) collective-permute-start(bf16[256,768]{1,0:T(8,128)(2,1)} %constant_dynamic-slice_fusion.14), channel_id=1, source_target_pairs={{1,2},{2,1},{5,6},{6,5},{9,10},{10,9},{13,14},{14,13},{17,18},{18,... | collective-permute-start | bytes 1179656 | tf_op jit(solution)/shard_map/ppermute | solution.py:668
  59.5 70.2 %collective-permute-start.9 = (bf16[2,96,768]{2,1,0:T(8,128)(2,1)}, bf16[2,96,768]{2,1,0:T(8,128)(2,1)}, u32[]{:S(2)}, u32[]{:S(2)}) collective-permute-start(bf16[2,96,768]{2,1,0:T(8,128)(2,1)} %pad_maximum_fusion.11), channel_id=1, source_target_pairs={{0,2},{2,0},{1,3},{3,1},{4,6},{6,4},{5,7},{7,5},{8,10},{10,8},{9,1... | collective-permute-start | bytes 884744 | tf_op jit(solution)/shard_map/ppermute | solution.py:602
  61.5 10.7 %collective-permute-start.4 = (bf16[192,1152]{1,0:T(8,128)(2,1)}, bf16[192,1152]{1,0:T(8,128)(2,1)S(1)}, u32[]{:S(2)}, u32[]{:S(2)}) collective-permute-start(bf16[192,1152]{1,0:T(8,128)(2,1)} %collective-permute-done.3.refs_0_), channel_id=1, source_target_pairs={{0,4},{4,0},{1,5},{5,1},{2,6},{6,2},{3,7},{7,3},{8,12},{12,8},{9,1... | collective-permute-start | bytes 1327112 | tf_op jit(solution)/shard_map/ppermute | solution.py:602
  66.2 35.8 %collective-permute-start.1 = (bf16[2,256,768]{2,1,0:T(8,128)(2,1)S(1)}, bf16[2,256,768]{2,1,0:T(8,128)(2,1)S(1)}, u32[]{:S(2)}, u32[]{:S(2)}) collective-permute-start(bf16[2,256,768]{2,1,0:T(8,128)(2,1)S(1)} %pad_maximum_fusion.8), channel_id=1, source_target_pairs={{0,2},{3,1},{4,6},{7,5},{8,10},{11,9},{12,14},{15,13},{16,18},{19,... | collective-permute-start | bytes 2359304 | tf_op jit(solution)/shard_map/ppermute | solution.py:627
  67.9 16.9 %collective-permute-start.11 = (bf16[768,384]{1,0:T(8,128)(2,1)}, bf16[768,384]{1,0:T(8,128)(2,1)S(1)}, u32[]{:S(2)}, u32[]{:S(2)}) collective-permute-start(bf16[768,384]{1,0:T(8,128)(2,1)} %collective-permute-done.10.u0.refs_0_), channel_id=1, source_target_pairs={{0,4},{4,0},{1,5},{5,1},{2,6},{6,2},{3,7},{7,3},{8,12},{12,8},{9,1... | collective-permute-start | bytes 1769480 | tf_op jit(solution)/shard_map/ppermute | solution.py:602
  68.2 29.2 %collective-permute-start.14 = (bf16[384,768]{1,0:T(8,128)(2,1)}, bf16[384,768]{1,0:T(8,128)(2,1)S(1)}, u32[]{:S(2)}, u32[]{:S(2)}) collective-permute-start(bf16[384,768]{1,0:T(8,128)(2,1)} %collective-permute-done.13.d0.refs_3_), channel_id=1, source_target_pairs={{0,4},{4,0},{1,5},{5,1},{2,6},{6,2},{3,7},{7,3},{8,12},{12,8},{9,1... | collective-permute-start | bytes 1769480 | tf_op jit(solution)/shard_map/ppermute | solution.py:602
  74.3 41.9 %collective-permute-start.5 = (bf16[2,192,1152]{2,1,0:T(8,128)(2,1)}, bf16[2,192,1152]{2,1,0:T(8,128)(2,1)}, u32[]{:S(2)}, u32[]{:S(2)}) collective-permute-start(bf16[2,192,1152]{2,1,0:T(8,128)(2,1)} %pad_maximum_fusion.7), channel_id=1, source_target_pairs={{0,2},{2,0},{1,3},{3,1},{4,6},{6,4},{5,7},{7,5},{8,10},{10,8},{9,1... | collective-permute-start | bytes 2654216 | tf_op jit(solution)/shard_map/ppermute | solution.py:602
  86.2 61.0 %collective-permute-start.12 = (bf16[2,768,384]{2,1,0:T(8,128)(2,1)S(1)}, bf16[2,768,384]{2,1,0:T(8,128)(2,1)}, u32[]{:S(2)}, u32[]{:S(2)}) collective-permute-start(bf16[2,768,384]{2,1,0:T(8,128)(2,1)S(1)} %pad_maximum_fusion.2), channel_id=1, source_target_pairs={{0,2},{2,0},{1,3},{3,1},{4,6},{6,4},{5,7},{7,5},{8,10},{10,8},{9,1... | collective-permute-start | bytes 3538952 | tf_op jit(solution)/shard_map/ppermute | solution.py:602
  99.8 47.5 %collective-permute-start.15 = (bf16[2,384,768]{2,1,0:T(8,128)(2,1)}, bf16[2,384,768]{2,1,0:T(8,128)(2,1)}, u32[]{:S(2)}, u32[]{:S(2)}) collective-permute-start(bf16[2,384,768]{2,1,0:T(8,128)(2,1)} %pad_maximum_fusion.3), channel_id=1, source_target_pairs={{0,2},{2,0},{1,3},{3,1},{4,6},{6,4},{5,7},{7,5},{8,10},{10,8},{9,1... | collective-permute-start | bytes 3538952 | tf_op jit(solution)/shard_map/ppermute | solution.py:602
  226.6 19.9 %collective-permute-start.21 = (bf16[2,192,1536]{2,1,0:T(8,128)(2,1)}, bf16[2,192,1536]{2,1,0:T(8,128)(2,1)S(1)}, u32[]{:S(2)}, u32[]{:S(2)}) collective-permute-start(bf16[2,192,1536]{2,1,0:T(8,128)(2,1)} %bitcast.105), channel_id=1, source_target_pairs={{0,2},{2,0},{1,3},{3,1},{4,6},{6,4},{5,7},{7,5},{8,10},{10,8},{9,1... | collective-permute-start | bytes 3538952 | tf_op jit(solution)/shard_map/ppermute | solution.py:602
  245.9 39.8 %collective-permute-start.20 = (bf16[2,192,1536]{2,1,0:T(8,128)(2,1)}, bf16[2,192,1536]{2,1,0:T(8,128)(2,1)}, u32[]{:S(2)}, u32[]{:S(2)}) collective-permute-start(bf16[2,192,1536]{2,1,0:T(8,128)(2,1)} %bitcast.104), channel_id=1, source_target_pairs={{0,2},{2,0},{1,3},{3,1},{4,6},{6,4},{5,7},{7,5},{8,10},{10,8},{9,1... | collective-permute-start | bytes 3538952 | tf_op jit(solution)/shard_map/ppermute | solution.py:602
  247.7 40.4 %collective-permute-start.22 = (bf16[2,96,1536]{2,1,0:T(8,128)(2,1)}, bf16[2,96,1536]{2,1,0:T(8,128)(2,1)S(1)}, u32[]{:S(2)}, u32[]{:S(2)}) collective-permute-start(bf16[2,96,1536]{2,1,0:T(8,128)(2,1)} %get-tuple-element.149), channel_id=1, source_target_pairs={{0,1},{1,0},{2,3},{3,2},{4,5},{5,4},{6,7},{7,6},{8,9},{9,8},{10,11... | collective-permute-start | bytes 1769480 | tf_op jit(solution)/shard_map/ppermute | solution.py:602
  247.7 40.4 %collective-permute-start.28 = (bf16[2,96,1536]{2,1,0:T(8,128)(2,1)}, bf16[2,96,1536]{2,1,0:T(8,128)(2,1)S(1)}, u32[]{:S(2)}, u32[]{:S(2)}) collective-permute-start(bf16[2,96,1536]{2,1,0:T(8,128)(2,1)} %get-tuple-element.150), channel_id=1, source_target_pairs={{0,1},{1,0},{2,3},{3,2},{4,5},{5,4},{6,7},{7,6},{8,9},{9,8},{10,11... | collective-permute-start | bytes 1769480 | tf_op jit(solution)/shard_map/ppermute | solution.py:602
  254.7 21.9 %collective-permute-start.38 = (f32[12,768]{1,0:T(8,128)S(1)}, f32[12,768]{1,0:T(8,128)S(1)}, u32[]{:S(2)}, u32[]{:S(2)}) collective-permute-start(f32[12,768]{1,0:T(8,128)S(1)} %add.338), channel_id=1, source_target_pairs={{0,1},{1,0},{2,3},{3,2},{4,5},{5,4},{6,7},{7,6},{8,9},{9,8},{10,11... | collective-permute-start | bytes 110600 | tf_op jit(solution)/shard_map/ppermute | solution.py:602
  280.9 35.9 %collective-permute-start.43 = (bf16[2,1536,384]{2,1,0:T(8,128)(2,1)}, bf16[2,1536,384]{2,1,0:T(8,128)(2,1)S(1)}, u32[]{:S(2)}, u32[]{:S(2)}) collective-permute-start(bf16[2,1536,384]{2,1,0:T(8,128)(2,1)} %get-tuple-element.130), channel_id=1, source_target_pairs={{0,2},{2,0},{1,3},{3,1},{4,6},{6,4},{5,7},{7,5},{8,10},{10,8},{9,1... | collective-permute-start | bytes 7077896 | tf_op jit(solution)/shard_map/ppermute | solution.py:602
  283.2 45.6 %collective-permute-start.42 = (bf16[2,1536,384]{2,1,0:T(8,128)(2,1)}, bf16[2,1536,384]{2,1,0:T(8,128)(2,1)}, u32[]{:S(2)}, u32[]{:S(2)}) collective-permute-start(bf16[2,1536,384]{2,1,0:T(8,128)(2,1)} %get-tuple-element.128), channel_id=1, source_target_pairs={{0,2},{2,0},{1,3},{3,1},{4,6},{6,4},{5,7},{7,5},{8,10},{10,8},{9,1... | collective-permute-start | bytes 7077896 | tf_op jit(solution)/shard_map/ppermute | solution.py:602
  285.7 32.9 %collective-permute-start.41 = (f32[12,768]{1,0:T(8,128)S(1)}, f32[12,768]{1,0:T(8,128)S(1)}, u32[]{:S(2)}, u32[]{:S(2)}) collective-permute-start(f32[12,768]{1,0:T(8,128)S(1)} %add.341), channel_id=1, source_target_pairs={{0,16},{8,24},{16,0},{24,8},{1,17},{9,25},{17,1},{25,9},{2,18},{10... | collective-permute-start | bytes 110600 | tf_op jit(solution)/shard_map/ppermute | solution.py:875
  289.8 8.4 %collective-permute-start.23 = (bf16[96,1536]{1,0:T(8,128)(2,1)S(1)}, bf16[96,1536]{1,0:T(8,128)(2,1)S(1)}, u32[]{:S(2)}, u32[]{:S(2)}) collective-permute-start(bf16[96,1536]{1,0:T(8,128)(2,1)S(1)} %slice_bitcast_fusion.12), channel_id=1, source_target_pairs={{0,4},{4,0},{1,5},{5,1},{2,6},{6,2},{3,7},{7,3},{8,12},{12,8},{9,1... | collective-permute-start | bytes 884744 | tf_op jit(solution)/shard_map/ppermute | solution.py:602
  290.2 14.4 %collective-permute-start.29 = (bf16[96,1536]{1,0:T(8,128)(2,1)S(1)}, bf16[96,1536]{1,0:T(8,128)(2,1)S(1)}, u32[]{:S(2)}, u32[]{:S(2)}) collective-permute-start(bf16[96,1536]{1,0:T(8,128)(2,1)S(1)} %slice_bitcast_fusion.10), channel_id=1, source_target_pairs={{0,4},{4,0},{1,5},{5,1},{2,6},{6,2},{3,7},{7,3},{8,12},{12,8},{9,1... | collective-permute-start | bytes 884744 | tf_op jit(solution)/shard_map/ppermute | solution.py:602
  298.3 7.7 %collective-permute-start.24 = (bf16[48,1536]{1,0:T(8,128)(2,1)S(1)}, bf16[48,1536]{1,0:T(8,128)(2,1)S(1)}, u32[]{:S(2)}, u32[]{:S(2)}) collective-permute-start(bf16[48,1536]{1,0:T(8,128)(2,1)S(1)} %constant_dynamic-slice_fusion.13), channel_id=1, source_target_pairs={{0,8},{8,0},{16,24},{24,16},{1,9},{9,1},{17,25},{25,17},{2,10},{10... | collective-permute-start | bytes 442376 | tf_op jit(solution)/shard_map/ppermute | solution.py:773
  314.5 7.2 %collective-permute-start.32 = (bf16[24,1536]{1,0:T(8,128)(2,1)S(1)}, bf16[24,1536]{1,0:T(8,128)(2,1)S(1)}, u32[]{:S(2)}, u32[]{:S(2)}) collective-permute-start(bf16[24,1536]{1,0:T(8,128)(2,1)S(1)} %add_convert_fusion.22), channel_id=1, source_target_pairs={{0,16},{8,24},{16,0},{24,8},{1,17},{9,25},{17,1},{25,9},{2,18},{10... | collective-permute-start | bytes 221192 | tf_op jit(solution)/shard_map/ppermute | solution.py:779
  316.7 6.3 %collective-permute-start.27 = (bf16[48,1536]{1,0:T(8,128)(2,1)S(1)}, bf16[48,1536]{1,0:T(8,128)(2,1)S(1)}, u32[]{:S(2)}, u32[]{:S(2)}) collective-permute-start(bf16[48,1536]{1,0:T(8,128)(2,1)S(1)} %maximum_select_fusion.8), channel_id=1, source_target_pairs={{0,8},{8,0},{16,24},{24,16},{1,9},{9,1},{17,25},{25,17},{2,10},{10... | collective-permute-start | bytes 442376 | tf_op jit(solution)/shard_map/ppermute | solution.py:779
  318.6 16.2 %collective-permute-start.44 = (bf16[2,384,384]{2,1,0:T(8,128)(2,1)}, bf16[2,384,384]{2,1,0:T(8,128)(2,1)}, u32[]{:S(2)}, u32[]{:S(2)}) collective-permute-start(bf16[2,384,384]{2,1,0:T(8,128)(2,1)} %get-tuple-element.143), channel_id=1, source_target_pairs={{0,1},{1,0},{2,3},{3,2},{4,5},{5,4},{6,7},{7,6},{8,9},{9,8},{10,11... | collective-permute-start | bytes 1769480 | tf_op jit(solution)/shard_map/ppermute | solution.py:602
  318.7 24.8 %collective-permute-start.50 = (bf16[2,384,384]{2,1,0:T(8,128)(2,1)}, bf16[2,384,384]{2,1,0:T(8,128)(2,1)}, u32[]{:S(2)}, u32[]{:S(2)}) collective-permute-start(bf16[2,384,384]{2,1,0:T(8,128)(2,1)} %get-tuple-element.146), channel_id=1, source_target_pairs={{0,1},{1,0},{2,3},{3,2},{4,5},{5,4},{6,7},{7,6},{8,9},{9,8},{10,11... | collective-permute-start | bytes 1769480 | tf_op jit(solution)/shard_map/ppermute | solution.py:602
  321.7 31.0 %collective-permute-start.56 = (bf16[2,384,384]{2,1,0:T(8,128)(2,1)}, bf16[2,384,384]{2,1,0:T(8,128)(2,1)}, u32[]{:S(2)}, u32[]{:S(2)}) collective-permute-start(bf16[2,384,384]{2,1,0:T(8,128)(2,1)} %get-tuple-element.145), channel_id=1, source_target_pairs={{0,1},{1,0},{2,3},{3,2},{4,5},{5,4},{6,7},{7,6},{8,9},{9,8},{10,11... | collective-permute-start | bytes 1769480 | tf_op jit(solution)/shard_map/ppermute | solution.py:602
  323.7 41.6 %collective-permute-start.62 = (bf16[2,384,384]{2,1,0:T(8,128)(2,1)}, bf16[2,384,384]{2,1,0:T(8,128)(2,1)}, u32[]{:S(2)}, u32[]{:S(2)}) collective-permute-start(bf16[2,384,384]{2,1,0:T(8,128)(2,1)} %get-tuple-element.144), channel_id=1, source_target_pairs={{0,1},{1,0},{2,3},{3,2},{4,5},{5,4},{6,7},{7,6},{8,9},{9,8},{10,11... | collective-permute-start | bytes 1769480 | tf_op jit(solution)/shard_map/ppermute | solution.py:602
  328.8 147.6 %collective-permute-start.18 = (bf16[256,768]{1,0:T(8,128)(2,1)}, bf16[256,768]{1,0:T(8,128)(2,1)}, u32[]{:S(2)}, u32[]{:S(2)}) collective-permute-start(bf16[256,768]{1,0:T(8,128)(2,1)} %slice.378), channel_id=1, source_target_pairs={{0,2},{2,0},{1,3},{3,1},{4,6},{6,4},{5,7},{7,5},{8,10},{10,8},{9,1... | collective-permute-start | bytes 1179656 | tf_op jit(solution)/shard_map/ppermute | solution.py:602
  334.8 144.9 %collective-permute-start.17 = (bf16[256,768]{1,0:T(8,128)(2,1)}, bf16[256,768]{1,0:T(8,128)(2,1)}, u32[]{:S(2)}, u32[]{:S(2)}) collective-permute-start(bf16[256,768]{1,0:T(8,128)(2,1)} %slice.217), channel_id=1, source_target_pairs={{1,2},{2,1},{5,6},{6,5},{9,10},{10,9},{13,14},{14,13},{17,18},{18,... | collective-permute-start | bytes 1179656 | tf_op jit(solution)/shard_map/ppermute | solution.py:668
  370.0 7.4 %collective-permute-start.51 = (bf16[384,384]{1,0:T(8,128)(2,1)S(1)}, bf16[384,384]{1,0:T(8,128)(2,1)S(1)}, u32[]{:S(2)}, u32[]{:S(2)}) collective-permute-start(bf16[384,384]{1,0:T(8,128)(2,1)S(1)} %slice_bitcast_fusion.6), channel_id=1, source_target_pairs={{0,4},{4,0},{1,5},{5,1},{2,6},{6,2},{3,7},{7,3},{8,12},{12,8},{9,1... | collective-permute-start | bytes 884744 | tf_op jit(solution)/shard_map/ppermute | solution.py:602
  370.3 10.3 %collective-permute-start.57 = (bf16[384,384]{1,0:T(8,128)(2,1)S(1)}, bf16[384,384]{1,0:T(8,128)(2,1)S(1)}, u32[]{:S(2)}, u32[]{:S(2)}) collective-permute-start(bf16[384,384]{1,0:T(8,128)(2,1)S(1)} %slice_bitcast_fusion.4), channel_id=1, source_target_pairs={{0,4},{4,0},{1,5},{5,1},{2,6},{6,2},{3,7},{7,3},{8,12},{12,8},{9,1... | collective-permute-start | bytes 884744 | tf_op jit(solution)/shard_map/ppermute | solution.py:602
  374.2 12.5 %collective-permute-start.63 = (bf16[384,384]{1,0:T(8,128)(2,1)S(1)}, bf16[384,384]{1,0:T(8,128)(2,1)S(1)}, u32[]{:S(2)}, u32[]{:S(2)}) collective-permute-start(bf16[384,384]{1,0:T(8,128)(2,1)S(1)} %slice_bitcast_fusion.2), channel_id=1, source_target_pairs={{0,4},{4,0},{1,5},{5,1},{2,6},{6,2},{3,7},{7,3},{8,12},{12,8},{9,1... | collective-permute-start | bytes 884744 | tf_op jit(solution)/shard_map/ppermute | solution.py:602
  377.4 12.0 %collective-permute-start.46 = (bf16[192,384]{1,0:T(8,128)(2,1)S(1)}, bf16[192,384]{1,0:T(8,128)(2,1)S(1)}, u32[]{:S(2)}, u32[]{:S(2)}) collective-permute-start(bf16[192,384]{1,0:T(8,128)(2,1)S(1)} %constant_dynamic-slice_fusion.7), channel_id=1, source_target_pairs={{0,8},{8,0},{16,24},{24,16},{1,9},{9,1},{17,25},{25,17},{2,10},{10... | collective-permute-start | bytes 442376 | tf_op jit(solution)/shard_map/ppermute | solution.py:773
  380.6 9.0 %collective-permute-start.52 = (bf16[192,384]{1,0:T(8,128)(2,1)S(1)}, bf16[192,384]{1,0:T(8,128)(2,1)S(1)}, u32[]{:S(2)}, u32[]{:S(2)}) collective-permute-start(bf16[192,384]{1,0:T(8,128)(2,1)S(1)} %constant_dynamic-slice_fusion.5), channel_id=1, source_target_pairs={{0,8},{8,0},{16,24},{24,16},{1,9},{9,1},{17,25},{25,17},{2,10},{10... | collective-permute-start | bytes 442376 | tf_op jit(solution)/shard_map/ppermute | solution.py:773
  386.8 11.7 %collective-permute-start.58 = (bf16[192,384]{1,0:T(8,128)(2,1)S(1)}, bf16[192,384]{1,0:T(8,128)(2,1)S(1)}, u32[]{:S(2)}, u32[]{:S(2)}) collective-permute-start(bf16[192,384]{1,0:T(8,128)(2,1)S(1)} %constant_dynamic-slice_fusion.3), channel_id=1, source_target_pairs={{0,8},{8,0},{16,24},{24,16},{1,9},{9,1},{17,25},{25,17},{2,10},{10... | collective-permute-start | bytes 442376 | tf_op jit(solution)/shard_map/ppermute | solution.py:773
  389.4 11.9 %collective-permute-start.64 = (bf16[192,384]{1,0:T(8,128)(2,1)S(1)}, bf16[192,384]{1,0:T(8,128)(2,1)S(1)}, u32[]{:S(2)}, u32[]{:S(2)}) collective-permute-start(bf16[192,384]{1,0:T(8,128)(2,1)S(1)} %constant_dynamic-slice_fusion.1), channel_id=1, source_target_pairs={{0,8},{8,0},{16,24},{24,16},{1,9},{9,1},{17,25},{25,17},{2,10},{10... | collective-permute-start | bytes 442376 | tf_op jit(solution)/shard_map/ppermute | solution.py:773
  389.5 15.0 %collective-permute-start.47 = (bf16[96,384]{1,0:T(8,128)(2,1)S(1)}, bf16[96,384]{1,0:T(8,128)(2,1)S(1)}, u32[]{:S(2)}, u32[]{:S(2)}) collective-permute-start(bf16[96,384]{1,0:T(8,128)(2,1)S(1)} %constant_dynamic-slice_fusion.6), channel_id=1, source_target_pairs={{0,16},{8,24},{16,0},{24,8},{1,17},{9,25},{17,1},{25,9},{2,18},{10... | collective-permute-start | bytes 221192 | tf_op jit(solution)/shard_map/ppermute | solution.py:773
  398.5 6.2 %collective-permute-start.53 = (bf16[96,384]{1,0:T(8,128)(2,1)S(1)}, bf16[96,384]{1,0:T(8,128)(2,1)S(1)}, u32[]{:S(2)}, u32[]{:S(2)}) collective-permute-start(bf16[96,384]{1,0:T(8,128)(2,1)S(1)} %constant_dynamic-slice_fusion.4), channel_id=1, source_target_pairs={{0,16},{8,24},{16,0},{24,8},{1,17},{9,25},{17,1},{25,9},{2,18},{10... | collective-permute-start | bytes 221192 | tf_op jit(solution)/shard_map/ppermute | solution.py:773
  401.2 5.9 %collective-permute-start.59 = (bf16[96,384]{1,0:T(8,128)(2,1)S(1)}, bf16[96,384]{1,0:T(8,128)(2,1)S(1)}, u32[]{:S(2)}, u32[]{:S(2)}) collective-permute-start(bf16[96,384]{1,0:T(8,128)(2,1)S(1)} %constant_dynamic-slice_fusion.2), channel_id=1, source_target_pairs={{0,16},{8,24},{16,0},{24,8},{1,17},{9,25},{17,1},{25,9},{2,18},{10... | collective-permute-start | bytes 221192 | tf_op jit(solution)/shard_map/ppermute | solution.py:773
  404.6 5.8 %collective-permute-start.65 = (bf16[96,384]{1,0:T(8,128)(2,1)S(1)}, bf16[96,384]{1,0:T(8,128)(2,1)S(1)}, u32[]{:S(2)}, u32[]{:S(2)}) collective-permute-start(bf16[96,384]{1,0:T(8,128)(2,1)S(1)} %constant_dynamic-slice_fusion), channel_id=1, source_target_pairs={{0,16},{8,24},{16,0},{24,8},{1,17},{9,25},{17,1},{25,9},{2,18},{10... | collective-permute-start | bytes 221192 | tf_op jit(solution)/shard_map/ppermute | solution.py:773
  404.7 11.8 %collective-permute-start.48 = (bf16[96,384]{1,0:T(8,128)(2,1)S(1)}, bf16[96,384]{1,0:T(8,128)(2,1)S(1)}, u32[]{:S(2)}, u32[]{:S(2)}) collective-permute-start(bf16[96,384]{1,0:T(8,128)(2,1)S(1)} %add_convert_fusion.21), channel_id=1, source_target_pairs={{0,16},{8,24},{16,0},{24,8},{1,17},{9,25},{17,1},{25,9},{2,18},{10... | collective-permute-start | bytes 221192 | tf_op jit(solution)/shard_map/ppermute | solution.py:779
  407.1 11.7 %collective-permute-start.54 = (bf16[96,384]{1,0:T(8,128)(2,1)S(1)}, bf16[96,384]{1,0:T(8,128)(2,1)S(1)}, u32[]{:S(2)}, u32[]{:S(2)}) collective-permute-start(bf16[96,384]{1,0:T(8,128)(2,1)S(1)} %add_convert_fusion.20), channel_id=1, source_target_pairs={{0,16},{8,24},{16,0},{24,8},{1,17},{9,25},{17,1},{25,9},{2,18},{10... | collective-permute-start | bytes 221192 | tf_op jit(solution)/shard_map/ppermute | solution.py:779
  410.3 10.1 %collective-permute-start.60 = (bf16[96,384]{1,0:T(8,128)(2,1)S(1)}, bf16[96,384]{1,0:T(8,128)(2,1)S(1)}, u32[]{:S(2)}, u32[]{:S(2)}) collective-permute-start(bf16[96,384]{1,0:T(8,128)(2,1)S(1)} %add_convert_fusion.19), channel_id=1, source_target_pairs={{0,16},{8,24},{16,0},{24,8},{1,17},{9,25},{17,1},{25,9},{2,18},{10... | collective-permute-start | bytes 221192 | tf_op jit(solution)/shard_map/ppermute | solution.py:779
  416.4 7.2 %collective-permute-start.66 = (bf16[96,384]{1,0:T(8,128)(2,1)S(1)}, bf16[96,384]{1,0:T(8,128)(2,1)S(1)}, u32[]{:S(2)}, u32[]{:S(2)}) collective-permute-start(bf16[96,384]{1,0:T(8,128)(2,1)S(1)} %add_convert_fusion.18), channel_id=1, source_target_pairs={{0,16},{8,24},{16,0},{24,8},{1,17},{9,25},{17,1},{25,9},{2,18},{10... | collective-permute-start | bytes 221192 | tf_op jit(solution)/shard_map/ppermute | solution.py:779
  418.8 6.2 %collective-permute-start.49 = (bf16[192,384]{1,0:T(8,128)(2,1)S(1)}, bf16[192,384]{1,0:T(8,128)(2,1)S(1)}, u32[]{:S(2)}, u32[]{:S(2)}) collective-permute-start(bf16[192,384]{1,0:T(8,128)(2,1)S(1)} %maximum_select_fusion.10), channel_id=1, source_target_pairs={{0,8},{8,0},{16,24},{24,16},{1,9},{9,1},{17,25},{25,17},{2,10},{10... | collective-permute-start | bytes 442376 | tf_op jit(solution)/shard_map/ppermute | solution.py:779
  420.4 6.4 %collective-permute-start.55 = (bf16[192,384]{1,0:T(8,128)(2,1)S(1)}, bf16[192,384]{1,0:T(8,128)(2,1)S(1)}, u32[]{:S(2)}, u32[]{:S(2)}) collective-permute-start(bf16[192,384]{1,0:T(8,128)(2,1)S(1)} %maximum_select_fusion.11), channel_id=1, source_target_pairs={{0,8},{8,0},{16,24},{24,16},{1,9},{9,1},{17,25},{25,17},{2,10},{10... | collective-permute-start | bytes 442376 | tf_op jit(solution)/shard_map/ppermute | solution.py:779
  423.6 6.6 %collective-permute-start.61 = (bf16[192,384]{1,0:T(8,128)(2,1)S(1)}, bf16[192,384]{1,0:T(8,128)(2,1)S(1)}, u32[]{:S(2)}, u32[]{:S(2)}) collective-permute-start(bf16[192,384]{1,0:T(8,128)(2,1)S(1)} %maximum_select_fusion.12), channel_id=1, source_target_pairs={{0,8},{8,0},{16,24},{24,16},{1,9},{9,1},{17,25},{25,17},{2,10},{10... | collective-permute-start | bytes 442376 | tf_op jit(solution)/shard_map/ppermute | solution.py:779
  425.0 8.5 %collective-permute-start.67 = (bf16[192,384]{1,0:T(8,128)(2,1)S(1)}, bf16[192,384]{1,0:T(8,128)(2,1)S(1)}, u32[]{:S(2)}, u32[]{:S(2)}) collective-permute-start(bf16[192,384]{1,0:T(8,128)(2,1)S(1)} %maximum_select_fusion.13), channel_id=1, source_target_pairs={{0,8},{8,0},{16,24},{24,16},{1,9},{9,1},{17,25},{25,17},{2,10},{10... | collective-permute-start | bytes 442376 | tf_op jit(solution)/shard_map/ppermute | solution.py:779
  426.8 8.3 %collective-permute-start.68 = (bf16[384,384]{1,0:T(8,128)(2,1)S(1)}, bf16[384,384]{1,0:T(8,128)(2,1)S(1)}, u32[]{:S(2)}, u32[]{:S(2)}) collective-permute-start(bf16[384,384]{1,0:T(8,128)(2,1)S(1)} %maximum_select_fusion.4), channel_id=1, source_target_pairs={{0,4},{4,0},{1,5},{5,1},{2,6},{6,2},{3,7},{7,3},{8,12},{12,8},{9,1... | collective-permute-start | bytes 884744 | tf_op jit(solution)/shard_map/ppermute | solution.py:602
  430.2 6.2 %collective-permute-start.69 = (bf16[384,384]{1,0:T(8,128)(2,1)S(1)}, bf16[384,384]{1,0:T(8,128)(2,1)S(1)}, u32[]{:S(2)}, u32[]{:S(2)}) collective-permute-start(bf16[384,384]{1,0:T(8,128)(2,1)S(1)} %maximum_select_fusion.5), channel_id=1, source_target_pairs={{0,4},{4,0},{1,5},{5,1},{2,6},{6,2},{3,7},{7,3},{8,12},{12,8},{9,1... | collective-permute-start | bytes 884744 | tf_op jit(solution)/shard_map/ppermute | solution.py:602
  433.5 6.6 %collective-permute-start.70 = (bf16[384,384]{1,0:T(8,128)(2,1)S(1)}, bf16[384,384]{1,0:T(8,128)(2,1)S(1)}, u32[]{:S(2)}, u32[]{:S(2)}) collective-permute-start(bf16[384,384]{1,0:T(8,128)(2,1)S(1)} %maximum_select_fusion.6), channel_id=1, source_target_pairs={{0,4},{4,0},{1,5},{5,1},{2,6},{6,2},{3,7},{7,3},{8,12},{12,8},{9,1... | collective-permute-start | bytes 884744 | tf_op jit(solution)/shard_map/ppermute | solution.py:602
  435.1 11.4 %collective-permute-start.71 = (bf16[384,384]{1,0:T(8,128)(2,1)S(1)}, bf16[384,384]{1,0:T(8,128)(2,1)S(1)}, u32[]{:S(2)}, u32[]{:S(2)}) collective-permute-start(bf16[384,384]{1,0:T(8,128)(2,1)S(1)} %maximum_select_fusion.7), channel_id=1, source_target_pairs={{0,4},{4,0},{1,5},{5,1},{2,6},{6,2},{3,7},{7,3},{8,12},{12,8},{9,1... | collective-permute-start | bytes 884744 | tf_op jit(solution)/shard_map/ppermute | solution.py:602
  436.4 24.2 %collective-permute-start.33 = (bf16[48,1536]{1,0:T(8,128)(2,1)S(1)}, bf16[48,1536]{1,0:T(8,128)(2,1)S(1)}, u32[]{:S(2)}, u32[]{:S(2)}) collective-permute-start(bf16[48,1536]{1,0:T(8,128)(2,1)S(1)} %maximum_select_fusion.9), channel_id=1, source_target_pairs={{0,8},{8,0},{16,24},{24,16},{1,9},{9,1},{17,25},{25,17},{2,10},{10... | collective-permute-start | bytes 442376 | tf_op jit(solution)/shard_map/ppermute | solution.py:779
  440.1 21.7 %collective-permute-start.34 = (bf16[96,1536]{1,0:T(8,128)(2,1)S(1)}, bf16[96,1536]{1,0:T(8,128)(2,1)S(1)}, u32[]{:S(2)}, u32[]{:S(2)}) collective-permute-start(bf16[96,1536]{1,0:T(8,128)(2,1)S(1)} %maximum_select_fusion.2), channel_id=1, source_target_pairs={{0,4},{4,0},{1,5},{5,1},{2,6},{6,2},{3,7},{7,3},{8,12},{12,8},{9,1... | collective-permute-start | bytes 884744 | tf_op jit(solution)/shard_map/ppermute | solution.py:602
  448.3 45.8 %collective-permute-start.72 = (bf16[2,1536,384]{2,1,0:T(8,128)(2,1)}, bf16[2,1536,384]{2,1,0:T(8,128)(2,1)}, u32[]{:S(2)}, u32[]{:S(2)}) collective-permute-start(bf16[2,1536,384]{2,1,0:T(8,128)(2,1)} %pad_maximum_fusion), channel_id=1, source_target_pairs={{0,2},{2,0},{1,3},{3,1},{4,6},{6,4},{5,7},{7,5},{8,10},{10,8},{9,1... | collective-permute-start | bytes 7077896 | tf_op jit(solution)/shard_map/ppermute | solution.py:602
  460.6 8.7 %collective-permute-start.35 = (bf16[96,1536]{1,0:T(8,128)(2,1)S(1)}, bf16[96,1536]{1,0:T(8,128)(2,1)S(1)}, u32[]{:S(2)}, u32[]{:S(2)}) collective-permute-start(bf16[96,1536]{1,0:T(8,128)(2,1)S(1)} %maximum_select_fusion.3), channel_id=1, source_target_pairs={{0,4},{4,0},{1,5},{5,1},{2,6},{6,2},{3,7},{7,3},{8,12},{12,8},{9,1... | collective-permute-start | bytes 884744 | tf_op jit(solution)/shard_map/ppermute | solution.py:602
  470.6 19.3 %collective-permute-start.36 = (bf16[2,192,1536]{2,1,0:T(8,128)(2,1)}, bf16[2,192,1536]{2,1,0:T(8,128)(2,1)}, u32[]{:S(2)}, u32[]{:S(2)}) collective-permute-start(bf16[2,192,1536]{2,1,0:T(8,128)(2,1)} %pad_maximum_fusion.5), channel_id=1, source_target_pairs={{0,2},{2,0},{1,3},{3,1},{4,6},{6,4},{5,7},{7,5},{8,10},{10,8},{9,1... | collective-permute-start | bytes 3538952 | tf_op jit(solution)/shard_map/ppermute | solution.py:602
  477.8 9.1 %collective-permute-start.19 = (bf16[256,768]{1,0:T(8,128)(2,1)S(1)}, bf16[256,768]{1,0:T(8,128)(2,1)S(1)}, u32[]{:S(2)}, u32[]{:S(2)}) collective-permute-start(bf16[256,768]{1,0:T(8,128)(2,1)S(1)} %fusion.6), channel_id=1, source_target_pairs={{1,2},{2,1},{5,6},{6,5},{9,10},{10,9},{13,14},{14,13},{17,18},{18,... | collective-permute-start | bytes 1179656 | tf_op jit(solution)/shard_map/ppermute | solution.py:668
  (41 other events, 275.5 us)
